TPU v7x, 32 devices: a whole 2x2x4 slice. The times are simulated.
32 devices in a mesh: feeder: 8 (over y, x, core), scen: 4 (over z).
Axes of the slice: x: 2, y: 2, z: 4, core: 2. Of those that a mesh axis runs over, the one named last changes fastest.
Arguments:
- anchor: bfloat16 [64, 24, 4096], P('scen', None, 'feeder'), may hold values from -6 to 6
- cost_lin: bfloat16 [64, 24, 4096], P('scen', None, 'feeder'), may hold values from -6 to 6
- dual: float32 [64, 24, 4096], P('scen', None, 'feeder'), may hold values from -4 to 4
- target: float32 [64, 24], P('scen'), may hold values from -4 to 4
- leaf_weight: float32 [64], P('scen'), may hold values from 1 to 10
- q_mat: bfloat16 [4096, 512], P('feeder'), may hold values from -0.25 to 0.25
- diag_gain: float32 [4096], P('feeder'), may hold values from 0.5 to 2
- block_mask: int32 [8, 4, 4], P('feeder'), may hold values from 0 to 1, as said below
- ancestor: int32 [24, 64], P(None, 'scen'), may hold values from 0 to 63, as said below
Outputs:
- setpoints: float32 [64, 24, 4096], P('scen', None, 'feeder')
- average: float32 [64, 24, 4096], P('scen', None, 'feeder')
- new_dual: float32 [64, 24, 4096], P('scen', None, 'feeder')
Inputs may be any that keep to these rules, and one draw needn't show every extreme that they name: `block_mask`: every diagonal block is present; the share of present off-diagonal blocks differs from feeder to feeder. ancestor[t, s] is the first leaf of the section-t tree node that holds leaf s: the leaves of a node are consecutive, ancestor[0, s] = 0, and every section-t node lies inside one section-(t-1) node. Nodes may span several groups at any section.
All inputs are finite; a program needn't handle non-finite values.
Results may differ from a plain program's by a relative error of at most 0.0003.
Values sent between devices are 32-bit elements; how exact they have to be, the bound alone decides.
A program may use at most 64 MiB of HBM per device.

v0:
```python
import jax
import jax.numpy as jnp
from jax import lax
from jax.sharding import PartitionSpec as P

PROX_ITERS = 8


penalty = 1.0
step_size = 0.08
coupling = 4.0
power_limit = 2.0


def entering(value, axis, combine, identity, reverse):
    length, here = (lax.axis_size(axis), lax.axis_index(axis))
    everything = jax.tree.map(lambda part: lax.all_gather(part, axis), value)
    start = jax.tree.map(
        lambda part, zero: jnp.broadcast_to(jnp.asarray(zero, part.dtype), part.shape),
        value,
        identity,
    )

    def hop(k, before):
        at = length - 1 - k if reverse else k
        reached = at > here if reverse else at < here
        new = combine(before, jax.tree.map(lambda part: part[at], everything))
        return jax.tree.map(lambda a, b: jnp.where(reached, a, b), new, before)

    return lax.fori_loop(0, length, hop, start)


def link_terms(earlier, later):
    return (
        later[0] + later[2][:, None] * earlier[0],
        later[1] + later[2] * earlier[1],
        earlier[2] * later[2],
    )


def local(anchor, cost_lin, dual, target, leaf_weight, q_mat, diag_gain, block_mask, ancestor):
    leaves, sections, nodes = anchor.shape
    rows = leaves * sections
    count = block_mask.shape[1]
    width = nodes // count
    total_nodes = lax.axis_size("feeder") * nodes
    start_pt = anchor.astype(jnp.float32)
    fixed_part = cost_lin.astype(jnp.float32) + dual - penalty * start_pt
    diag_term = 2.0 * diag_gain + penalty
    expand = jnp.repeat(jnp.repeat(block_mask[0], width, axis=0), width, axis=1).astype(
        jnp.bfloat16
    )
    q_eff = q_mat * expand
    state = start_pt
    for sweep in range(PROX_ITERS):
        flat = state.reshape(rows, nodes).astype(jnp.bfloat16)
        image = jnp.dot(flat, q_eff, preferred_element_type=jnp.float32)
        head = lax.psum(jnp.sum(state, axis=2), "feeder") / total_nodes
        grad = image.reshape(leaves, sections, nodes) + diag_term * state + fixed_part
        grad = grad + coupling * (head - target)[:, :, None]
        state = jnp.clip(state - step_size * grad, -power_limit, power_limit)
    highest = lax.Precision.HIGHEST
    weighted = leaf_weight[:, None, None] * state
    first_leaf = lax.axis_index("scen") * leaves
    local_id = jnp.maximum(ancestor - first_leaf, 0)
    slot_ids = jnp.arange(leaves, dtype=jnp.int32)
    member = (local_id[:, None, :] == slot_ids[None, :, None]).astype(jnp.float32)
    seg_sums = jnp.einsum("tgl,ltn->tgn", member, weighted, precision=highest)
    seg_weights = jnp.einsum("tgl,l->tg", member, leaf_weight, precision=highest)
    last_pick = (slot_ids[None, :] == local_id[:, leaves - 1][:, None]).astype(jnp.float32)
    first_pick = (slot_ids[None, :] == 0).astype(jnp.float32)
    tail_sum = jnp.einsum("tg,tgn->tn", last_pick, seg_sums, precision=highest)
    tail_weight = jnp.sum(last_pick * seg_weights, axis=1)
    continued = (ancestor[:, 0] < first_leaf).astype(jnp.float32)
    spanning = (ancestor[:, leaves - 1] < first_leaf).astype(jnp.float32)
    head_sum = seg_sums[:, 0, :] * continued[:, None]
    head_weight = seg_weights[:, 0] * continued
    blank = (jnp.zeros_like(tail_sum), jnp.zeros_like(tail_weight), jnp.ones_like(spanning))
    before = entering((tail_sum, tail_weight, spanning), "scen", link_terms, blank, False)
    after = entering((head_sum, head_weight, spanning), "scen", link_terms, blank, True)
    open_front = first_pick * continued[:, None]
    seg_total = (
        seg_sums
        + open_front[:, :, None] * before[0][:, None, :]
        + last_pick[:, :, None] * after[0][:, None, :]
    )
    weight_total = seg_weights + open_front * before[1][:, None] + last_pick * after[1][:, None]
    leaf_sums = jnp.einsum("tgl,tgn->ltn", member, seg_total, precision=highest)
    leaf_weights = jnp.einsum("tgl,tg->lt", member, weight_total, precision=highest)
    average = leaf_sums / leaf_weights[:, :, None]
    new_dual = dual + penalty * (state - average)
    return (state, average, new_dual)


def solution(mesh):
    return jax.shard_map(
        local,
        mesh=mesh,
        in_specs=(
            P("scen", None, "feeder"),
            P("scen", None, "feeder"),
            P("scen", None, "feeder"),
            P("scen", None),
            P("scen"),
            P("feeder", None),
            P("feeder"),
            P("feeder", None, None),
            P(None, "scen"),
        ),
        out_specs=(P("scen", None, "feeder"), P("scen", None, "feeder"), P("scen", None, "feeder")),
        check_vma=False,
    )
```

profile of v0, /device:TPU:0, one launch (start us, length us, event | category | flops | bytes accessed | tf_op | source)
XLA Modules:
  0.0 162.8 jit_solution(4398324740652846305)
XLA Ops:
  0.6 0.7 convert_bitcast_fusion
  2.1 0.9 copy-done
  3.9 15.5 %psum.56 = f32[16,24]{1,0:T(8,128)S(1)} all-reduce(f32[16,24]{1,0:T(8,128)S(1)} %convert_reduce_fusion), channel_id=1, replica_groups=mesh['feeder'=8,'scen'=4] {'feeder'}, use_global_device_ids=true, to_apply=%region_1.0 | all-reduce | flops 384 | bytes 3072 | tf_op jit(solution)/shard_map/psum | solution.py:58
  19.4 1.4 fusion.74
  20.8 12.1 %psum.57 = f32[16,24]{1,0:T(8,128)S(1)} all-reduce(f32[16,24]{1,0:T(8,128)S(1)} %get-tuple-element.401), channel_id=1, replica_groups=mesh['feeder'=8,'scen'=4] {'feeder'}, use_global_device_ids=true, to_apply=%region_3.4 | all-reduce | flops 384 | bytes 3072 | tf_op jit(solution)/shard_map/psum | solution.py:58
  32.9 0.9 fusion.93
  33.8 12.1 %psum.58 = f32[16,24]{1,0:T(8,128)S(1)} all-reduce(f32[16,24]{1,0:T(8,128)S(1)} %get-tuple-element.407), channel_id=1, replica_groups=mesh['feeder'=8,'scen'=4] {'feeder'}, use_global_device_ids=true, to_apply=%region_5.6 | all-reduce | flops 384 | bytes 3072 | tf_op jit(solution)/shard_map/psum | solution.py:58
  46.5 12.1 %psum.59 = f32[16,24]{1,0:T(8,128)S(1)} all-reduce(f32[16,24]{1,0:T(8,128)S(1)} %get-tuple-element.409), channel_id=1, replica_groups=mesh['feeder'=8,'scen'=4] {'feeder'}, use_global_device_ids=true, to_apply=%region_7.8 | all-reduce | flops 384 | bytes 3072 | tf_op jit(solution)/shard_map/psum | solution.py:58
  59.2 12.1 %psum.60 = f32[16,24]{1,0:T(8,128)S(1)} all-reduce(f32[16,24]{1,0:T(8,128)S(1)} %get-tuple-element.411), channel_id=1, replica_groups=mesh['feeder'=8,'scen'=4] {'feeder'}, use_global_device_ids=true, to_apply=%region_9.10 | all-reduce | flops 384 | bytes 3072 | tf_op jit(solution)/shard_map/psum | solution.py:58
  71.9 12.1 %psum.61 = f32[16,24]{1,0:T(8,128)S(1)} all-reduce(f32[16,24]{1,0:T(8,128)S(1)} %get-tuple-element.413), channel_id=1, replica_groups=mesh['feeder'=8,'scen'=4] {'feeder'}, use_global_device_ids=true, to_apply=%region_11.12 | all-reduce | flops 384 | bytes 3072 | tf_op jit(solution)/shard_map/psum | solution.py:58
  84.1 1.4 fusion.97
  85.4 12.1 %psum.62 = f32[16,24]{1,0:T(8,128)S(1)} all-reduce(f32[16,24]{1,0:T(8,128)S(1)} %get-tuple-element.415), channel_id=1, replica_groups=mesh['feeder'=8,'scen'=4] {'feeder'}, use_global_device_ids=true, to_apply=%region_13.14 | all-reduce | flops 384 | bytes 3072 | tf_op jit(solution)/shard_map/psum | solution.py:58
  97.5 2.0 %fusion.98 = (f32[16,24]{1,0:T(8,128)S(1)}, f32[16,24,512]{2,1,0:T(8,128)S(1)}) fusion(f32[16,24,512]{2,1,0:T(8,128)} %get-tuple-element.416, f32[16,24]{1,0:T(8,128)S(1)} %subtract_multiply_fusion.1, f32[16,24,512]{2,1,0:T(8,128)S(1)} %get-tuple-element.402, f32[512]{0:T(512)S(1)} %multiply_add_fusion, bf16[512,512]{1,0:T(8,128)(2,1)S(1)} %bitcast_multiply_fusion), kind=kOutput, calls=%fused_computation.144 | convolution fusion | flops 203095680 | bytes 2888704 | tf_op jit(solution)/shard_map/dot_general | solution.py:57
  99.5 12.1 %psum.63 = f32[16,24]{1,0:T(8,128)S(1)} all-reduce(f32[16,24]{1,0:T(8,128)S(1)} %get-tuple-element.417), channel_id=1, replica_groups=mesh['feeder'=8,'scen'=4] {'feeder'}, use_global_device_ids=true, to_apply=%region_15.16 | all-reduce | flops 384 | bytes 3072 | tf_op jit(solution)/shard_map/psum | solution.py:58
  111.7 0.6 copy-done.8
  112.3 1.4 broadcast_multiply_fusion
  113.7 0.7 copy-done.6
  114.5 1.0 fusion.48
  116.1 13.9 %all-gather = f32[96,512]{1,0:T(8,128)S(1)} all-gather(f32[24,512]{1,0:T(8,128)S(1)} %bitcast.116), channel_id=2, replica_groups=mesh['feeder'=8,'scen'=4] {'scen'}, dimensions={0}, use_global_device_ids=true | all-gather | bytes 245760 | tf_op jit(solution)/shard_map/all_gather | solution.py:17
  130.3 0.6 copy-done.9
  132.6 12.2 %all-reduce.3 = (f32[96]{0:T(128)S(1)}, f32[96]{0:T(128)S(1)}, f32[96]{0:T(128)S(1)}) all-reduce(f32[96]{0:T(128)S(1)} %fusion.86, f32[96]{0:T(128)S(1)} %fusion.84, f32[96]{0:T(128)S(1)} %dynamic-update-slice.1), channel_id=3, replica_groups=mesh['feeder'=8,'scen'=4] {'scen'}, use_global_device_ids=true, to_apply=%add | all-reduce | flops 288 | bytes 2304
  145.5 13.6 %all_gather.31 = f32[4,24,512]{2,1,0:T(8,128)S(1)} all-gather(f32[1,24,512]{2,1,0:T(8,128)S(1)} %copy.24), channel_id=1, replica_groups=mesh['feeder'=8,'scen'=4] {'scen'}, dimensions={0}, use_global_device_ids=true | all-gather | bytes 245760 | tf_op jit(solution)/shard_map/all_gather | solution.py:17
  159.8 0.7 fusion.50
  161.2 1.7 %subtract_add_fusion = (f32[16,24,512]{2,1,0:T(8,128)}, f32[16,24,512]{2,1,0:T(8,128)}) fusion(f32[16,24,512]{2,1,0:T(8,128)S(1)} %copy-done.3, f32[16,24,512]{2,1,0:T(8,128)S(1)} %copy-done.1, f32[16,24]{1,0:T(8,128)S(1)} %bitcast.118, f32[24,512,16]{1,2,0:T(8,128)S(1)} %fusion.50), kind=kLoop, calls=%fused_computation.72 | loop fusion | flops 589824 | bytes 3933696 | tf_op jit(solution)/shard_map/add | solution.py:91
  (85 shorter events, 8.0 us)
Async XLA Ops:
  0.6 1.4 copy-start.4
  2.0 1.0 copy-start
  3.0 0.7 copy-start.7
  3.0 16.3 %copy-start.2 = (f32[16,24,512]{2,1,0:T(8,128)S(1)}, f32[16,24,512]{2,1,0:T(8,128)}, u32[]{:S(2)}) copy-start(f32[16,24,512]{2,1,0:T(8,128)} %param.15) | copy-start | bytes 2359300
  3.8 15.5 %copy-start.5 = (f32[16,24]{1,0:T(8,128)S(1)}, f32[16,24]{1,0:T(8,128)}, u32[]{:S(2)}) copy-start(f32[16,24]{1,0:T(8,128)} %param.16) | copy-start | bytes 4612
  111.7 0.7 copy-start.8
  113.7 0.7 copy-start.6
  130.3 0.7 copy-start.9
  159.8 1.1 copy-start.1
  159.8 1.4 copy-start.3
where the time goes:
time: 163 us
  blocking collectives  140 us (86%)
  matrix products  10.1 us (6%)
  local copies, waits for them, and re-layouts  5.79 us (4%)
  other arithmetic  5.4 us (3%)
    psum x8, blocking collectives, local(): head = lax.psum(jnp.sum(state, axis=2), 'feeder') / total_nodes  100 us
    all_gather x2, blocking collectives, entering(): everything = jax.tree.map(lambda part: lax.all_gather(part, axis), value)  27.5 us
    unnamed x1, blocking collectives  12.2 us
    dot_general x8, matrix products, local(): image = jnp.dot(flat, q_eff, preferred_element_type=jnp.float32)  7.69 us
    unnamed x26, local copies, waits for them, and re-layouts  4.45 us

commit v1 on v0

v1 whole, which is shorter than its diff:
```python
import functools

import jax
import jax.numpy as jnp
from jax import lax
from jax.experimental import pallas as pl
from jax.experimental.pallas import tpu as pltpu
from jax.sharding import PartitionSpec as P

PROX_ITERS = 8

penalty = 1.0
step_size = 0.08
coupling = 4.0
power_limit = 2.0

LANES = 128
MESH = pl.DeviceIdType.MESH
F32 = jnp.float32
BF16 = jnp.bfloat16


def kernel(
    nf, ns,
    anchor_hbm, cost_hbm, dual_hbm, q_hbm, target_ref, weight_ref, diag_ref, mask_ref, anc_ref,
    x_hbm, avg_hbm, newdual_hbm,
    anchor_v, cost_v, dual_v, q_v, nat, fixed_nat, xt, pre, fixed_t, q_t, gain_t, head_col,
    x_out, avg_out, dual_out, total, same, inv, from_left, from_right,
    head_send, head_recv, note_send, note_recv, up_send, up_recv, down_send, down_recv, tail, front,
    in_sem, out_sem, head_ssem, head_rsem, note_ssem, note_rsem, up_ssem, up_rsem, down_ssem, down_rsem,
):
    leaves, sections, nodes = x_hbm.shape
    rows = leaves * sections
    lane_blocks = rows // LANES
    node_blocks = nodes // LANES
    mf, ms = lax.axis_index("feeder"), lax.axis_index("scen")

    barrier = pltpu.get_barrier_semaphore()
    for k in range(1, nf):
        pl.semaphore_signal(barrier, inc=1, device_id=(lax.rem(mf + k, nf), ms), device_id_type=MESH)
    for k in range(1, ns):
        pl.semaphore_signal(barrier, inc=1, device_id=(mf, lax.rem(ms + k, ns)), device_id_type=MESH)
    loads = [
        pltpu.make_async_copy(src, dst, in_sem.at[i])
        for i, (src, dst) in enumerate(
            ((anchor_hbm, anchor_v), (q_hbm, q_v), (cost_hbm, cost_v), (dual_hbm, dual_v))
        )
    ]
    for load in loads:
        load.start()

    def leaf_rows(leaf):
        return pl.ds(leaf * sections, sections)

    def lanes(block):
        return pl.ds(block * LANES, LANES)

    def send_heads(step):
        for k in range(1, nf):
            pltpu.make_async_remote_copy(
                src_ref=head_send.at[step],
                dst_ref=head_recv.at[step, k - 1],
                send_sem=head_ssem.at[step],
                recv_sem=head_rsem.at[step],
                device_id=(lax.rem(mf + k, nf), ms),
                device_id_type=MESH,
            ).start()

    def head_term(step):
        got = head_recv.at[step]
        pltpu.make_async_copy(got, got, head_rsem.at[step]).wait()
        pltpu.make_async_copy(got, got, head_ssem.at[step]).wait()
        whole = head_send[step]
        for k in range(nf - 1):
            whole = whole + head_recv[step, k]
        return whole * (step_size * coupling / (nf * nodes))

    def window():
        image = jnp.dot(q_t[...], xt[...].astype(BF16), preferred_element_type=F32)
        for b in range(lane_blocks):
            cols = slice(b * LANES, (b + 1) * LANES)
            pre[:, cols] = gain_t[...] * xt[:, cols] - step_size * image[:, cols] - fixed_t[:, cols]

    loads[0].wait()
    for leaf in range(leaves):
        nat[leaf_rows(leaf), :] = anchor_v[leaf].astype(F32)
    for b in range(lane_blocks):
        block = nat[lanes(b), :].T
        xt[:, lanes(b)] = block
        head_send[0, :, lanes(b)] = jnp.sum(block, axis=0, keepdims=True)
    pl.semaphore_wait(barrier, nf - 1 + ns - 1)
    send_heads(0)

    wide = (sections, LANES)
    ids = [jnp.broadcast_to(anc_ref[:, l : l + 1].astype(F32), wide) for l in range(leaves)]
    run_w = [jnp.full(wide, weight_ref[0], F32)]
    for l in range(1, leaves):
        link = (ids[l] == ids[l - 1]).astype(F32)
        same[l] = link
        run_w.append(link * run_w[-1] + weight_ref[l])
    total_w = [None] * leaves
    total_w[leaves - 1] = run_w[leaves - 1]
    for l in range(leaves - 2, -1, -1):
        total_w[l] = jnp.where(ids[l] == ids[l + 1], total_w[l + 1], run_w[l])
    for l in range(leaves):
        inv[l] = total_w[l]
    column = lax.broadcasted_iota(jnp.int32, wide, 1)
    note_send[...] = jnp.where(
        column == 0,
        run_w[leaves - 1],
        jnp.where(column == 1, ids[leaves - 1], jnp.where(column == 2, total_w[0], ids[0])),
    )
    for k in range(1, ns):
        pltpu.make_async_remote_copy(
            src_ref=note_send,
            dst_ref=note_recv.at[k - 1],
            send_sem=note_ssem,
            recv_sem=note_rsem,
            device_id=(mf, lax.rem(ms + k, ns)),
            device_id_type=MESH,
        ).start()

    loads[1].wait()
    for i in range(node_blocks):
        for j in range(node_blocks):
            keep = mask_ref[0, i, j].astype(F32)
            q_t[lanes(j), lanes(i)] = (q_v[lanes(i), lanes(j)].astype(F32) * keep).T.astype(BF16)
    gain_t[...] = 1.0 - step_size * (
        2.0 * jnp.broadcast_to(diag_ref[...], (LANES, nodes)).T + penalty
    )
    loads[2].wait()
    loads[3].wait()
    diagonal = lax.broadcasted_iota(jnp.int32, (sections, sections), 0) == lax.broadcasted_iota(
        jnp.int32, (sections, sections), 1
    )
    for l in range(leaves):
        goal = jnp.broadcast_to(target_ref[l : l + 1, :], (sections, sections))
        goal = jnp.sum(jnp.where(diagonal, goal, 0.0), axis=1, keepdims=True)
        fixed_nat[leaf_rows(l), :] = step_size * (
            cost_v[l].astype(F32) + dual_v[l] - penalty * nat[leaf_rows(l), :] - coupling * goal
        )
    for b in range(lane_blocks):
        fixed_t[:, lanes(b)] = fixed_nat[lanes(b), :].T
    window()

    def advance(step, carry):
        term = head_term(step - 1)
        part = jnp.zeros((8, rows), F32)
        for b in range(nodes // 64):
            some = slice(b * 64, (b + 1) * 64)
            new = jnp.clip(pre[some, :] - term, -power_limit, power_limit)
            xt[some, :] = new
            part = part + jnp.sum(new.reshape(8, 8, rows), axis=0)
        head_send[step] = jnp.sum(part, axis=0, keepdims=True)
        send_heads(step)
        window()
        return carry

    lax.fori_loop(1, 3, advance, 0)

    pltpu.make_async_copy(note_recv, note_recv, note_rsem).wait()
    pltpu.make_async_copy(note_recv, note_recv, note_ssem).wait()
    first_id = jnp.broadcast_to(anc_ref[:, 0:1].astype(F32), wide)
    last_id = jnp.broadcast_to(anc_ref[:, leaves - 1 : leaves].astype(F32), wide)
    start = (ms * leaves).astype(F32)
    goes_back = (first_id < start).astype(F32)
    spans = (last_id < start).astype(F32)
    left_w = jnp.zeros(wide, F32)
    right_w = jnp.zeros(wide, F32)
    for k in range(1, ns):
        note = note_recv[k - 1]
        earlier = jnp.where(ms >= k, 1.0, 0.0)
        left_w += earlier * jnp.where(note[:, 1:2] == first_id, note[:, 0:1], 0.0)
        right_w += (1.0 - earlier) * jnp.where(note[:, 3:4] == last_id, note[:, 2:3], 0.0)
    for l in range(leaves):
        own_id = jnp.broadcast_to(anc_ref[:, l : l + 1].astype(F32), wide)
        in_first = (own_id == first_id).astype(F32)
        in_last = (own_id == last_id).astype(F32)
        scale = 1.0 / (inv[l] + in_first * left_w + in_last * right_w)
        inv[l] = scale
        from_left[l] = in_first * goes_back * scale
        from_right[l] = in_last * scale

    lax.fori_loop(3, PROX_ITERS, advance, 0)

    for b in range(lane_blocks):
        nat[lanes(b), :] = pre[:, lanes(b)].T
    term = head_term(PROX_ITERS - 1)
    for b in range(lane_blocks):
        head_col[lanes(b), :] = jnp.broadcast_to(term[:, b * LANES : (b + 1) * LANES], (LANES, LANES)).T

    def up_copy(c):
        return pltpu.make_async_remote_copy(
            src_ref=up_send.at[c], dst_ref=up_recv.at[c],
            send_sem=up_ssem.at[c], recv_sem=up_rsem.at[c],
            device_id=(mf, lax.rem(ms + 1, ns)), device_id_type=MESH,
        )

    def down_copy(c):
        return pltpu.make_async_remote_copy(
            src_ref=down_send.at[c], dst_ref=down_recv.at[c],
            send_sem=down_ssem.at[c], recv_sem=down_rsem.at[c],
            device_id=(mf, lax.rem(ms + ns - 1, ns)), device_id_type=MESH,
        )

    at_bottom, at_top = ms == 0, ms == ns - 1
    for c in range(node_blocks):
        run = None
        for l in range(leaves):
            x = jnp.clip(nat[leaf_rows(l), lanes(c)] - head_col[leaf_rows(l), :], -power_limit, power_limit)
            x_out[l, :, lanes(c)] = x
            weighted = weight_ref[l] * x
            if l == 0:
                run = weighted
                opening = weighted
                in_first = goes_back
            else:
                run = weighted + same[l] * run
                in_first = in_first * same[l]
                opening = opening + in_first * weighted
            total[l, :, lanes(c)] = run
        opening = opening * goes_back
        tail[c] = run
        front[c] = opening

        @pl.when(at_bottom)
        def _():
            up_send[c] = run
            up_copy(c).start()

        @pl.when(at_top)
        def _():
            down_send[c] = opening
            down_copy(c).start()

    store_x = pltpu.make_async_copy(x_out, x_hbm, out_sem.at[0])
    store_x.start()

    for c in range(node_blocks):
        after = total[leaves - 1, :, lanes(c)]
        for l in range(leaves - 2, -1, -1):
            after = jnp.where(same[l + 1] > 0.5, after, total[l, :, lanes(c)])
            total[l, :, lanes(c)] = after

    def upward():
        for c in range(node_blocks):
            up_copy(c).wait_recv()

            @pl.when(jnp.logical_not(at_top))
            def _():
                up_send[c] = tail[c] + spans * up_recv[c]
                up_copy(c).start()

    def downward():
        for c in range(node_blocks):
            down_copy(c).wait_recv()

            @pl.when(jnp.logical_not(at_bottom))
            def _():
                down_send[c] = front[c] + spans * down_recv[c]
                down_copy(c).start()

    low = ms < ns // 2

    @pl.when(at_bottom)
    def _():
        up_recv[...] = jnp.zeros_like(up_recv)

    @pl.when(at_top)
    def _():
        down_recv[...] = jnp.zeros_like(down_recv)

    @pl.when(jnp.logical_and(low, jnp.logical_not(at_bottom)))
    def _():
        upward()

    @pl.when(jnp.logical_not(at_top))
    def _():
        downward()

    @pl.when(jnp.logical_not(low))
    def _():
        upward()

    stores = []
    for l in range(leaves):
        for c in range(node_blocks):
            average = (
                total[l, :, lanes(c)] * inv[l] + from_left[l] * up_recv[c] + from_right[l] * down_recv[c]
            )
            avg_out[l, :, lanes(c)] = average
            dual_out[l, :, lanes(c)] = dual_v[l, :, lanes(c)] + penalty * (x_out[l, :, lanes(c)] - average)
        if l % 4 == 3:
            done = pl.ds(l - 3, 4)
            for i, (src, dst) in enumerate(((avg_out, avg_hbm), (dual_out, newdual_hbm))):
                store = pltpu.make_async_copy(src.at[done], dst.at[done], out_sem.at[1 + 2 * (l // 4) + i])
                store.start()
                stores.append(store)
    for c in range(node_blocks):

        @pl.when(jnp.logical_not(at_top))
        def _():
            up_copy(c).wait_send()

        @pl.when(jnp.logical_not(at_bottom))
        def _():
            down_copy(c).wait_send()

    store_x.wait()
    for store in stores:
        store.wait()


def local(nf, ns, anchor, cost_lin, dual, target, leaf_weight, q_mat, diag_gain, block_mask, ancestor):
    leaves, sections, nodes = anchor.shape
    rows = leaves * sections
    blocks = nodes // LANES
    vmem, smem = pltpu.VMEM, pltpu.SMEM
    dma = pltpu.SemaphoreType.DMA
    cube = (leaves, sections, nodes)
    coef = (leaves, sections, LANES)
    piece = (blocks, sections, LANES)
    out = jax.ShapeDtypeStruct(cube, F32)
    far = pl.BlockSpec(memory_space=pl.ANY)
    near = pl.BlockSpec(memory_space=vmem)
    scalars = pl.BlockSpec(memory_space=smem)
    return pl.pallas_call(
        functools.partial(kernel, nf, ns),
        out_shape=(out, out, out),
        in_specs=[far, far, far, far, near, scalars, near, scalars, near],
        out_specs=(far, far, far),
        scratch_shapes=[
            vmem(cube, BF16), vmem(cube, BF16), vmem(cube, F32), vmem((nodes, nodes), BF16),
            vmem((rows, nodes), F32), vmem((rows, nodes), F32),
            vmem((nodes, rows), F32), vmem((nodes, rows), F32), vmem((nodes, rows), F32),
            vmem((nodes, nodes), BF16), vmem((nodes, LANES), F32), vmem((rows, LANES), F32),
            vmem(cube, F32), vmem(cube, F32), vmem(cube, F32), vmem(cube, F32),
            vmem(coef, F32), vmem(coef, F32), vmem(coef, F32), vmem(coef, F32),
            vmem((PROX_ITERS, 1, rows), F32), vmem((PROX_ITERS, nf - 1, 1, rows), F32),
            vmem((sections, LANES), F32), vmem((ns - 1, sections, LANES), F32),
            vmem(piece, F32), vmem(piece, F32), vmem(piece, F32), vmem(piece, F32),
            vmem(piece, F32), vmem(piece, F32),
            dma((4,)), dma((1 + leaves // 2,)), dma((PROX_ITERS,)), dma((PROX_ITERS,)), dma, dma,
            dma((blocks,)), dma((blocks,)), dma((blocks,)), dma((blocks,)),
        ],
        compiler_params=pltpu.CompilerParams(
            collective_id=0, has_side_effects=True, vmem_limit_bytes=56 * 1024 * 1024
        ),
        cost_estimate=pl.CostEstimate(
            flops=2 * PROX_ITERS * rows * nodes * nodes, bytes_accessed=24 * rows * nodes, transcendentals=0
        ),
    )(anchor, cost_lin, dual, q_mat, target, leaf_weight, diag_gain.reshape(1, nodes), block_mask, ancestor)


def solution(mesh):
    return jax.shard_map(
        functools.partial(local, mesh.shape["feeder"], mesh.shape["scen"]),
        mesh=mesh,
        in_specs=(
            P("scen", None, "feeder"),
            P("scen", None, "feeder"),
            P("scen", None, "feeder"),
            P("scen", None),
            P("scen"),
            P("feeder", None),
            P("feeder"),
            P("feeder", None, None),
            P(None, "scen"),
        ),
        out_specs=(P("scen", None, "feeder"), P("scen", None, "feeder"), P("scen", None, "feeder")),
        check_vma=False,
    )
```

time: 163 us -> 48.5 us (0.30)
  blocking collectives: 140 us -> 0 us
  Pallas kernels: 0 us -> 41.7 us
  matrix products: 10.1 us -> 0 us
  other arithmetic: 5.4 us -> 0 us
    psum x8 -> x0, blocking collectives: 100 us -> none  [local(): head = lax.psum(jnp.sum(state, axis=2), 'feeder') / total_nodes]
    pallas_call x0 -> x1, Pallas kernels: none -> 41.7 us  [local(): pl.pallas_call(functools.partial(kernel, nf, ns), out_shape=(out, out, ou...]
    all_gather x2 -> x0, blocking collectives: 27.5 us -> none  [entering(): everything = jax.tree.map(lambda part: lax.all_gather(part, axis), value)]
    unnamed x1 -> x0, blocking collectives: 12.2 us -> none
    dot_general x12 -> x0, matrix products: 10.1 us -> none  [the longest x8 7.69 us: local(): image = jnp.dot(flat, q_eff, preferred_element_type=jnp.float32)]
    add x2 -> x0, other arithmetic: 1.67 us -> none  [the longest x1 1.66 us: local(): new_dual = dual + penalty * (state - average)]
    unnamed x26 -> x8, local copies, waits for them, and re-layouts: 4.45 us -> 5.81 us
where the time goes in v1:
time: 48.5 us; the launch traced here: 48.2 us
  Pallas kernels  41.7 us (86%)
  local copies, waits for them, and re-layouts  5.81 us (12%)
  between operations  0.65 us (1%)
    pallas_call x1, Pallas kernels, local(): pl.pallas_call(functools.partial(kernel, nf, ns), out_shape=(out, out, ou...  41.7 us
    unnamed x8, local copies, waits for them, and re-layouts  5.81 us

profile of v1, /device:TPU:0, one launch (start us, length us, event | category | flops | bytes accessed | tf_op | source)
XLA Modules:
  0.0 48.2 jit_solution(4394785707824576867)
XLA Ops:
  0.6 1.4 %copy.12.anc_ref = s32[24,16]{1,0:T(8,128)} copy(s32[24,16]{0,1:T(8,128)} %param.17) | data formatting | bytes 3072 | tf_op args[8]
  2.0 41.7 %shard_map.112 = (f32[16,24,512]{2,1,0:T(8,128)}, f32[16,24,512]{2,1,0:T(8,128)}, f32[16,24,512]{2,1,0:T(8,128)}) custom-call(bf16[16,24,512]{2,1,0:T(8,128)(2,1)} %anchor_hbm.1, bf16[16,24,512]{2,1,0:T(8,128)(2,1)} %cost_hbm.1, f32[16,24,512]{2,1,0:T(8,128)} %dual_hbm.1, bf16[512,512]{1,0:T(8,128)(2,1)} %q_hbm.1, f32[16,24]{1,0:T(8,128)} %target_ref.1, ...), custom_call_target="tpu_custom_call" | custom-call | flops 1610612736 | bytes 4718592 | tf_op jit(solution)/shard_map/pallas_call | solution.py:327
  43.7 0.0 copy-start.1
  43.7 2.1 %copy.16 = f32[16,24,512]{2,1,0:T(8,128)} copy(f32[16,24,512]{2,1,0:T(8,128)} %get-tuple-element.6) | data formatting | bytes 1572864
  45.9 0.0 copy-done.1
  45.9 0.0 copy-start
  45.9 0.9 %copy.17 = f32[16,24,512]{2,1,0:T(8,128)} copy(f32[16,24,512]{2,1,0:T(8,128)S(1)} %copy-done.1) | data formatting | bytes 1572864
  46.8 0.5 %copy-done = f32[16,24,512]{2,1,0:T(8,128)S(1)} copy-done((f32[16,24,512]{2,1,0:T(8,128)S(1)}, f32[16,24,512]{2,1,0:T(8,128)}, u32[]{:S(2)}) %copy-start) | copy-done | bytes 786456
  47.3 0.9 %copy.18 = f32[16,24,512]{2,1,0:T(8,128)} copy(f32[16,24,512]{2,1,0:T(8,128)S(1)} %copy-done) | data formatting | bytes 1572864
Async XLA Ops:
  43.7 2.2 %copy-start.1 = (f32[16,24,512]{2,1,0:T(8,128)S(1)}, f32[16,24,512]{2,1,0:T(8,128)}, u32[]{:S(2)}) copy-start(f32[16,24,512]{2,1,0:T(8,128)} %get-tuple-element.7) | copy-start | bytes 2359300
  45.9 1.4 %copy-start = (f32[16,24,512]{2,1,0:T(8,128)S(1)}, f32[16,24,512]{2,1,0:T(8,128)}, u32[]{:S(2)}) copy-start(f32[16,24,512]{2,1,0:T(8,128)} %get-tuple-element.8) | copy-start | bytes 2359300

commit v2 on v1

--- a/solution.py
+++ b/solution.py
@@ -23,9 +23,9 @@
 def kernel(
     nf, ns,
     anchor_hbm, cost_hbm, dual_hbm, q_hbm, target_ref, weight_ref, diag_ref, mask_ref, anc_ref,
-    x_hbm, avg_hbm, newdual_hbm,
+    x_hbm, packed_ref,
     anchor_v, cost_v, dual_v, q_v, nat, fixed_nat, xt, pre, fixed_t, q_t, gain_t, head_col,
-    x_out, avg_out, dual_out, total, same, inv, from_left, from_right,
+    x_out, small, total_w, same,
     head_send, head_recv, note_send, note_recv, up_send, up_recv, down_send, down_recv, tail, front,
     in_sem, out_sem, head_ssem, head_rsem, note_ssem, note_rsem, up_ssem, up_rsem, down_ssem, down_rsem,
 ):
@@ -92,23 +92,30 @@
     send_heads(0)
 
     wide = (sections, LANES)
-    ids = [jnp.broadcast_to(anc_ref[:, l : l + 1].astype(F32), wide) for l in range(leaves)]
+    small[...] = jnp.zeros_like(small)
+    small[0:leaves, 0:sections] = anc_ref[...].astype(F32)
+    small[leaves : 2 * leaves, 0:sections] = target_ref[...]
+    small[...] = small[...].T
+
+    def leaf_id(l):
+        return jnp.broadcast_to(small[0:sections, l : l + 1], wide)
+
+    ids = [leaf_id(l) for l in range(leaves)]
     run_w = [jnp.full(wide, weight_ref[0], F32)]
     for l in range(1, leaves):
         link = (ids[l] == ids[l - 1]).astype(F32)
         same[l] = link
         run_w.append(link * run_w[-1] + weight_ref[l])
-    total_w = [None] * leaves
-    total_w[leaves - 1] = run_w[leaves - 1]
+    own_w = run_w[leaves - 1]
+    total_w[leaves - 1] = own_w
     for l in range(leaves - 2, -1, -1):
-        total_w[l] = jnp.where(ids[l] == ids[l + 1], total_w[l + 1], run_w[l])
-    for l in range(leaves):
-        inv[l] = total_w[l]
+        own_w = jnp.where(ids[l] == ids[l + 1], own_w, run_w[l])
+        total_w[l] = own_w
     column = lax.broadcasted_iota(jnp.int32, wide, 1)
     note_send[...] = jnp.where(
         column == 0,
         run_w[leaves - 1],
-        jnp.where(column == 1, ids[leaves - 1], jnp.where(column == 2, total_w[0], ids[0])),
+        jnp.where(column == 1, ids[leaves - 1], jnp.where(column == 2, own_w, ids[0])),
     )
     for k in range(1, ns):
         pltpu.make_async_remote_copy(
@@ -130,12 +137,8 @@
     )
     loads[2].wait()
     loads[3].wait()
-    diagonal = lax.broadcasted_iota(jnp.int32, (sections, sections), 0) == lax.broadcasted_iota(
-        jnp.int32, (sections, sections), 1
-    )
     for l in range(leaves):
-        goal = jnp.broadcast_to(target_ref[l : l + 1, :], (sections, sections))
-        goal = jnp.sum(jnp.where(diagonal, goal, 0.0), axis=1, keepdims=True)
+        goal = small[0:sections, leaves + l : leaves + l + 1]
         fixed_nat[leaf_rows(l), :] = step_size * (
             cost_v[l].astype(F32) + dual_v[l] - penalty * nat[leaf_rows(l), :] - coupling * goal
         )
@@ -160,8 +163,8 @@
 
     pltpu.make_async_copy(note_recv, note_recv, note_rsem).wait()
     pltpu.make_async_copy(note_recv, note_recv, note_ssem).wait()
-    first_id = jnp.broadcast_to(anc_ref[:, 0:1].astype(F32), wide)
-    last_id = jnp.broadcast_to(anc_ref[:, leaves - 1 : leaves].astype(F32), wide)
+    first_id = leaf_id(0)
+    last_id = leaf_id(leaves - 1)
     start = (ms * leaves).astype(F32)
     goes_back = (first_id < start).astype(F32)
     spans = (last_id < start).astype(F32)
@@ -172,14 +175,18 @@
         earlier = jnp.where(ms >= k, 1.0, 0.0)
         left_w += earlier * jnp.where(note[:, 1:2] == first_id, note[:, 0:1], 0.0)
         right_w += (1.0 - earlier) * jnp.where(note[:, 3:4] == last_id, note[:, 2:3], 0.0)
+    packed = jnp.zeros(wide, F32)
     for l in range(leaves):
-        own_id = jnp.broadcast_to(anc_ref[:, l : l + 1].astype(F32), wide)
+        own_id = leaf_id(l)
         in_first = (own_id == first_id).astype(F32)
         in_last = (own_id == last_id).astype(F32)
-        scale = 1.0 / (inv[l] + in_first * left_w + in_last * right_w)
-        inv[l] = scale
-        from_left[l] = in_first * goes_back * scale
-        from_right[l] = in_last * scale
+        scale = 1.0 / (total_w[l] + in_first * left_w + in_last * right_w)
+        packed = jnp.where(column == l, scale, packed)
+        packed = jnp.where(column == leaves + l, in_first * goes_back * scale, packed)
+        packed = jnp.where(column == 2 * leaves + l, in_last * scale, packed)
+        if l > 0:
+            packed = jnp.where(column == 3 * leaves + l, same[l], packed)
+    packed_ref[2 * node_blocks] = packed
 
     lax.fori_loop(3, PROX_ITERS, advance, 0)
 
@@ -218,7 +225,6 @@
                 run = weighted + same[l] * run
                 in_first = in_first * same[l]
                 opening = opening + in_first * weighted
-            total[l, :, lanes(c)] = run
         opening = opening * goes_back
         tail[c] = run
         front[c] = opening
@@ -236,12 +242,6 @@
     store_x = pltpu.make_async_copy(x_out, x_hbm, out_sem.at[0])
     store_x.start()
 
-    for c in range(node_blocks):
-        after = total[leaves - 1, :, lanes(c)]
-        for l in range(leaves - 2, -1, -1):
-            after = jnp.where(same[l + 1] > 0.5, after, total[l, :, lanes(c)])
-            total[l, :, lanes(c)] = after
-
     def upward():
         for c in range(node_blocks):
             up_copy(c).wait_recv()
@@ -282,20 +282,9 @@
     def _():
         upward()
 
-    stores = []
-    for l in range(leaves):
-        for c in range(node_blocks):
-            average = (
-                total[l, :, lanes(c)] * inv[l] + from_left[l] * up_recv[c] + from_right[l] * down_recv[c]
-            )
-            avg_out[l, :, lanes(c)] = average
-            dual_out[l, :, lanes(c)] = dual_v[l, :, lanes(c)] + penalty * (x_out[l, :, lanes(c)] - average)
-        if l % 4 == 3:
-            done = pl.ds(l - 3, 4)
-            for i, (src, dst) in enumerate(((avg_out, avg_hbm), (dual_out, newdual_hbm))):
-                store = pltpu.make_async_copy(src.at[done], dst.at[done], out_sem.at[1 + 2 * (l // 4) + i])
-                store.start()
-                stores.append(store)
+    for c in range(node_blocks):
+        packed_ref[c] = up_recv[c]
+        packed_ref[node_blocks + c] = down_recv[c]
     for c in range(node_blocks):
 
         @pl.when(jnp.logical_not(at_top))
@@ -307,8 +296,59 @@
             down_copy(c).wait_send()
 
     store_x.wait()
-    for store in stores:
-        store.wait()
+
+
+def finish(
+    x_hbm, dual_hbm, packed_ref, weight_ref,
+    xout_hbm, avg_hbm, newdual_hbm,
+    x_v, dual_v, avg_v, new_v, coef, in_sem, out_sem,
+):
+    leaves, sections, nodes = x_hbm.shape
+    node_blocks = nodes // LANES
+
+    def lanes(block):
+        return pl.ds(block * LANES, LANES)
+
+    def load(c):
+        return [
+            pltpu.make_async_copy(src.at[:, :, lanes(c)], dst.at[:, :, lanes(c)], in_sem.at[2 * c + i])
+            for i, (src, dst) in enumerate(((x_hbm, x_v), (dual_hbm, dual_v)))
+        ]
+
+    def store(c):
+        return [
+            pltpu.make_async_copy(src.at[:, :, lanes(c)], dst.at[:, :, lanes(c)], out_sem.at[3 * c + i])
+            for i, (src, dst) in enumerate(((x_v, xout_hbm), (avg_v, avg_hbm), (new_v, newdual_hbm)))
+        ]
+
+    for c in range(node_blocks):
+        for copy in load(c):
+            copy.start()
+    packed = packed_ref[2 * node_blocks]
+    for i in range(4 * leaves):
+        coef[i] = jnp.broadcast_to(packed[:, i : i + 1], (sections, LANES))
+    scale, left, right, same = (lambda l, i=i: coef[i * leaves + l] for i in range(4))
+    for c in range(node_blocks):
+        from_x, from_dual = load(c)
+        from_x.wait()
+        run = weight_ref[0] * x_v[0, :, lanes(c)]
+        avg_v[0, :, lanes(c)] = run
+        for l in range(1, leaves):
+            run = weight_ref[l] * x_v[l, :, lanes(c)] + same(l) * run
+            avg_v[l, :, lanes(c)] = run
+        from_dual.wait()
+        total = run
+        for l in range(leaves - 1, -1, -1):
+            if l < leaves - 1:
+                total = jnp.where(same(l + 1) > 0.5, total, avg_v[l, :, lanes(c)])
+            average = total * scale(l) + left(l) * packed_ref[c] + right(l) * packed_ref[node_blocks + c]
+            avg_v[l, :, lanes(c)] = average
+            new_v[l, :, lanes(c)] = dual_v[l, :, lanes(c)] + penalty * (x_v[l, :, lanes(c)] - average)
+        for copy in store(c):
+            copy.start()
+    for c in range(node_blocks):
+        for copy in store(c):
+            copy.wait()
 
 
 def local(nf, ns, anchor, cost_lin, dual, target, leaf_weight, q_mat, diag_gain, block_mask, ancestor):
@@ -324,32 +364,46 @@
     far = pl.BlockSpec(memory_space=pl.ANY)
     near = pl.BlockSpec(memory_space=vmem)
     scalars = pl.BlockSpec(memory_space=smem)
-    return pl.pallas_call(
+    packed = jax.ShapeDtypeStruct((2 * blocks + 1, sections, LANES), F32)
+    limit = 56 * 1024 * 1024
+    state, parts = pl.pallas_call(
         functools.partial(kernel, nf, ns),
-        out_shape=(out, out, out),
+        out_shape=(out, packed),
         in_specs=[far, far, far, far, near, scalars, near, scalars, near],
-        out_specs=(far, far, far),
+        out_specs=(far, near),
         scratch_shapes=[
             vmem(cube, BF16), vmem(cube, BF16), vmem(cube, F32), vmem((nodes, nodes), BF16),
             vmem((rows, nodes), F32), vmem((rows, nodes), F32),
             vmem((nodes, rows), F32), vmem((nodes, rows), F32), vmem((nodes, rows), F32),
             vmem((nodes, nodes), BF16), vmem((nodes, LANES), F32), vmem((rows, LANES), F32),
-            vmem(cube, F32), vmem(cube, F32), vmem(cube, F32), vmem(cube, F32),
-            vmem(coef, F32), vmem(coef, F32), vmem(coef, F32), vmem(coef, F32),
+            vmem(cube, F32), vmem((LANES, LANES), F32),
+            vmem(coef, F32), vmem(coef, F32),
             vmem((PROX_ITERS, 1, rows), F32), vmem((PROX_ITERS, nf - 1, 1, rows), F32),
             vmem((sections, LANES), F32), vmem((ns - 1, sections, LANES), F32),
             vmem(piece, F32), vmem(piece, F32), vmem(piece, F32), vmem(piece, F32),
             vmem(piece, F32), vmem(piece, F32),
-            dma((4,)), dma((1 + leaves // 2,)), dma((PROX_ITERS,)), dma((PROX_ITERS,)), dma, dma,
+            dma((4,)), dma((1,)), dma((PROX_ITERS,)), dma((PROX_ITERS,)), dma, dma,
             dma((blocks,)), dma((blocks,)), dma((blocks,)), dma((blocks,)),
         ],
         compiler_params=pltpu.CompilerParams(
-            collective_id=0, has_side_effects=True, vmem_limit_bytes=56 * 1024 * 1024
+            collective_id=0, has_side_effects=True, vmem_limit_bytes=limit
         ),
         cost_estimate=pl.CostEstimate(
-            flops=2 * PROX_ITERS * rows * nodes * nodes, bytes_accessed=24 * rows * nodes, transcendentals=0
+            flops=2 * PROX_ITERS * rows * nodes * nodes, bytes_accessed=12 * rows * nodes, transcendentals=0
         ),
-    )(anchor, cost_lin, dual, q_mat, target, leaf_weight, diag_gain.reshape(1, nodes), block_mask, ancestor)
+    )(anchor, cost_lin, dual, q_mat, target, leaf_weight, diag_gain.reshape(1, nodes), block_mask, ancestor.T)
+    return pl.pallas_call(
+        finish,
+        out_shape=(out, out, out),
+        in_specs=[far, far, near, scalars],
+        out_specs=(far, far, far),
+        scratch_shapes=[
+            vmem(cube, F32), vmem(cube, F32), vmem(cube, F32), vmem(cube, F32),
+            vmem((4 * leaves, sections, LANES), F32), dma((2 * blocks,)), dma((3 * blocks,)),
+        ],
+        compiler_params=pltpu.CompilerParams(vmem_limit_bytes=limit),
+        cost_estimate=pl.CostEstimate(flops=10 * rows * nodes, bytes_accessed=20 * rows * nodes, transcendentals=0),
+    )(state, dual, parts, leaf_weight)
 
 
 def solution(mesh):

time: 48.5 us -> 45.5 us (0.938)
  local copies, waits for them, and re-layouts: 5.81 us -> 0 us
  Pallas kernels: 41.7 us -> 44.6 us
    unnamed x8 -> x0, local copies, waits for them, and re-layouts: 5.81 us -> none
    pallas_call x1 -> x2, Pallas kernels: 41.7 us -> 44.6 us  [the longest x1 41.1 us: local(): pl.pallas_call(functools.partial(kernel, nf, ns), out_shape=(out, packed)...]
where the time goes in v2:
time: 45.5 us; the launch traced here: 45.3 us
  Pallas kernels  44.6 us (98%)
  between operations  0.64 us (1%)
    pallas_call x1, Pallas kernels, local(): pl.pallas_call(functools.partial(kernel, nf, ns), out_shape=(out, packed)...  41.1 us
    pallas_call x1, Pallas kernels, local(): pl.pallas_call(finish, out_shape=(out, out, out), in_specs=[far, far, nea...  3.5 us

profile of v2, /device:TPU:0, one launch (start us, length us, event | category | flops | bytes accessed | tf_op | source)
XLA Modules:
  0.0 45.3 jit_solution(2259569488958065740)
XLA Ops:
  0.6 41.1 %shard_map.112 = (f32[16,24,512]{2,1,0:T(8,128)}, f32[9,24,128]{2,1,0:T(8,128)}) custom-call(bf16[16,24,512]{2,1,0:T(8,128)(2,1)} %anchor_hbm.1, bf16[16,24,512]{2,1,0:T(8,128)(2,1)} %cost_hbm.1, f32[16,24,512]{2,1,0:T(8,128)} %dual_hbm.3, bf16[512,512]{1,0:T(8,128)(2,1)} %q_hbm.1, f32[16,24]{1,0:T(8,128)} %target_ref.1, f32[16]{0:T(128)} %weight_ref.3, ...), custom_call_target="tpu_custom_call" | custom-call | flops 1610612736 | bytes 2359296 | tf_op jit(solution)/shard_map/pallas_call | solution.py:369
  41.8 3.5 %shard_map.113 = (f32[16,24,512]{2,1,0:T(8,128)}, f32[16,24,512]{2,1,0:T(8,128)}, f32[16,24,512]{2,1,0:T(8,128)}) custom-call(f32[16,24,512]{2,1,0:T(8,128)} %get-tuple-element.5.x_hbm, f32[16,24,512]{2,1,0:T(8,128)} %dual_hbm.3, f32[9,24,128]{2,1,0:T(8,128)} %get-tuple-element.6.packed_ref, f32[16]{0:T(128)} %weight_ref.3), custom_call_target="tpu_custom_call" | custom-call | flops 1966080 | bytes 3932160 | tf_op jit(solution)/shard_map/pallas_call | solution.py:395

commit v3 on v2

--- a/solution.py
+++ b/solution.py
@@ -24,7 +24,7 @@
     nf, ns,
     anchor_hbm, cost_hbm, dual_hbm, q_hbm, target_ref, weight_ref, diag_ref, mask_ref, anc_ref,
     x_hbm, packed_ref,
-    anchor_v, cost_v, dual_v, q_v, nat, fixed_nat, xt, pre, fixed_t, q_t, gain_t, head_col,
+    anchor_v, cost_v, dual_v, q_v, q_m, nat_b, nat, fixed_nat, xt, pre, fixed_t, q_t, gain_t, head_col,
     x_out, small, total_w, same,
     head_send, head_recv, note_send, note_recv, up_send, up_recv, down_send, down_recv, tail, front,
     in_sem, out_sem, head_ssem, head_rsem, note_ssem, note_rsem, up_ssem, up_rsem, down_ssem, down_rsem,
@@ -35,9 +35,19 @@
     node_blocks = nodes // LANES
     mf, ms = lax.axis_index("feeder"), lax.axis_index("scen")
 
+    def partner(k):
+        other, bit = mf, 1
+        while bit < nf:
+            if k & bit:
+                other = other + bit - 2 * bit * lax.rem(lax.div(mf, bit), 2)
+            bit *= 2
+        return other
+
+    order = sorted(range(1, nf), key=lambda k: -bin(k >> 1).count("1"))
+
     barrier = pltpu.get_barrier_semaphore()
     for k in range(1, nf):
-        pl.semaphore_signal(barrier, inc=1, device_id=(lax.rem(mf + k, nf), ms), device_id_type=MESH)
+        pl.semaphore_signal(barrier, inc=1, device_id=(partner(k), ms), device_id_type=MESH)
     for k in range(1, ns):
         pl.semaphore_signal(barrier, inc=1, device_id=(mf, lax.rem(ms + k, ns)), device_id_type=MESH)
     loads = [
@@ -56,13 +66,13 @@
         return pl.ds(block * LANES, LANES)
 
     def send_heads(step):
-        for k in range(1, nf):
+        for k in order:
             pltpu.make_async_remote_copy(
                 src_ref=head_send.at[step],
                 dst_ref=head_recv.at[step, k - 1],
                 send_sem=head_ssem.at[step],
                 recv_sem=head_rsem.at[step],
-                device_id=(lax.rem(mf + k, nf), ms),
+                device_id=(partner(k), ms),
                 device_id_type=MESH,
             ).start()
 
@@ -84,18 +94,62 @@
     loads[0].wait()
     for leaf in range(leaves):
         nat[leaf_rows(leaf), :] = anchor_v[leaf].astype(F32)
-    for b in range(lane_blocks):
-        block = nat[lanes(b), :].T
-        xt[:, lanes(b)] = block
-        head_send[0, :, lanes(b)] = jnp.sum(block, axis=0, keepdims=True)
+    nat_b[...] = nat[...].astype(BF16)
+    ones = jnp.ones((8, nodes), BF16)
+    sums = lax.dot_general(ones, nat_b[...], (((1,), (1,)), ((), ())), preferred_element_type=F32)
+    head_send[0] = sums[0:1, :]
     pl.semaphore_wait(barrier, nf - 1 + ns - 1)
     send_heads(0)
 
-    wide = (sections, LANES)
     small[...] = jnp.zeros_like(small)
     small[0:leaves, 0:sections] = anc_ref[...].astype(F32)
     small[leaves : 2 * leaves, 0:sections] = target_ref[...]
     small[...] = small[...].T
+    loads[1].wait()
+    for i in range(node_blocks):
+        for j in range(node_blocks):
+            q_m[lanes(i), lanes(j)] = q_v[lanes(i), lanes(j)] * mask_ref[0, i, j].astype(F32).astype(BF16)
+    loads[2].wait()
+    loads[3].wait()
+    image = jnp.dot(nat_b[...], q_m[...], preferred_element_type=F32)
+    gain_row = 1.0 - step_size * (2.0 * diag_ref[...] + penalty)
+    for l in range(leaves):
+        goal = small[0:sections, leaves + l : leaves + l + 1]
+        here = nat[leaf_rows(l), :]
+        fixed = step_size * (cost_v[l].astype(F32) + dual_v[l] - penalty * here - coupling * goal)
+        fixed_nat[leaf_rows(l), :] = fixed
+        nat[leaf_rows(l), :] = (
+            gain_row * here - step_size * image[l * sections : (l + 1) * sections, :] - fixed
+        )
+    for b in range(lane_blocks):
+        pre[:, lanes(b)] = nat[lanes(b), :].T
+
+    def update(step):
+        term = head_term(step - 1)
+        part = jnp.zeros((8, rows), F32)
+        for b in range(nodes // 64):
+            some = slice(b * 64, (b + 1) * 64)
+            new = jnp.clip(pre[some, :] - term, -power_limit, power_limit)
+            xt[some, :] = new
+            part = part + jnp.sum(new.reshape(8, 8, rows), axis=0)
+        head_send[step] = jnp.sum(part, axis=0, keepdims=True)
+        send_heads(step)
+
+    def advance(step, carry):
+        update(step)
+        window()
+        return carry
+
+    update(1)
+    q_t[...] = q_m[...].T
+    for b in range(lane_blocks):
+        fixed_t[:, lanes(b)] = fixed_nat[lanes(b), :].T
+    gain_t[...] = jnp.broadcast_to(gain_row, (LANES, nodes)).T
+    window()
+
+    advance(2, 0)
+
+    wide = (sections, LANES)
 
     def leaf_id(l):
         return jnp.broadcast_to(small[0:sections, l : l + 1], wide)
@@ -127,39 +181,7 @@
             device_id_type=MESH,
         ).start()
 
-    loads[1].wait()
-    for i in range(node_blocks):
-        for j in range(node_blocks):
-            keep = mask_ref[0, i, j].astype(F32)
-            q_t[lanes(j), lanes(i)] = (q_v[lanes(i), lanes(j)].astype(F32) * keep).T.astype(BF16)
-    gain_t[...] = 1.0 - step_size * (
-        2.0 * jnp.broadcast_to(diag_ref[...], (LANES, nodes)).T + penalty
-    )
-    loads[2].wait()
-    loads[3].wait()
-    for l in range(leaves):
-        goal = small[0:sections, leaves + l : leaves + l + 1]
-        fixed_nat[leaf_rows(l), :] = step_size * (
-            cost_v[l].astype(F32) + dual_v[l] - penalty * nat[leaf_rows(l), :] - coupling * goal
-        )
-    for b in range(lane_blocks):
-        fixed_t[:, lanes(b)] = fixed_nat[lanes(b), :].T
-    window()
-
-    def advance(step, carry):
-        term = head_term(step - 1)
-        part = jnp.zeros((8, rows), F32)
-        for b in range(nodes // 64):
-            some = slice(b * 64, (b + 1) * 64)
-            new = jnp.clip(pre[some, :] - term, -power_limit, power_limit)
-            xt[some, :] = new
-            part = part + jnp.sum(new.reshape(8, 8, rows), axis=0)
-        head_send[step] = jnp.sum(part, axis=0, keepdims=True)
-        send_heads(step)
-        window()
-        return carry
-
-    lax.fori_loop(1, 3, advance, 0)
+    lax.fori_loop(3, 5, advance, 0)
 
     pltpu.make_async_copy(note_recv, note_recv, note_rsem).wait()
     pltpu.make_async_copy(note_recv, note_recv, note_ssem).wait()
@@ -188,7 +210,7 @@
             packed = jnp.where(column == 3 * leaves + l, same[l], packed)
     packed_ref[2 * node_blocks] = packed
 
-    lax.fori_loop(3, PROX_ITERS, advance, 0)
+    lax.fori_loop(5, PROX_ITERS, advance, 0)
 
     for b in range(lane_blocks):
         nat[lanes(b), :] = pre[:, lanes(b)].T
@@ -373,7 +395,7 @@
         out_specs=(far, near),
         scratch_shapes=[
             vmem(cube, BF16), vmem(cube, BF16), vmem(cube, F32), vmem((nodes, nodes), BF16),
-            vmem((rows, nodes), F32), vmem((rows, nodes), F32),
+            vmem((nodes, nodes), BF16), vmem((rows, nodes), BF16), vmem((rows, nodes), F32), vmem((rows, nodes), F32),
             vmem((nodes, rows), F32), vmem((nodes, rows), F32), vmem((nodes, rows), F32),
             vmem((nodes, nodes), BF16), vmem((nodes, LANES), F32), vmem((rows, LANES), F32),
             vmem(cube, F32), vmem((LANES, LANES), F32),

time: 45.5 us -> 45.4 us (level)
  no operation moved by 1% of the time
where the time goes in v3:
time: 45.4 us; the launch traced here: 45.2 us
  Pallas kernels  44.5 us (98%)
  between operations  0.64 us (1%)
    pallas_call x1, Pallas kernels, local(): pl.pallas_call(functools.partial(kernel, nf, ns), out_shape=(out, packed)...  41 us
    pallas_call x1, Pallas kernels, local(): pl.pallas_call(finish, out_shape=(out, out, out), in_specs=[far, far, nea...  3.5 us

profile of v3, /device:TPU:0, one launch (start us, length us, event | category | flops | bytes accessed | tf_op | source)
XLA Modules:
  0.0 45.2 jit_solution(10716345760667867451)
XLA Ops:
  0.6 41.0 %shard_map.112 = (f32[16,24,512]{2,1,0:T(8,128)}, f32[9,24,128]{2,1,0:T(8,128)}) custom-call(bf16[16,24,512]{2,1,0:T(8,128)(2,1)} %anchor_hbm.1, bf16[16,24,512]{2,1,0:T(8,128)(2,1)} %cost_hbm.1, f32[16,24,512]{2,1,0:T(8,128)} %dual_hbm.3, bf16[512,512]{1,0:T(8,128)(2,1)} %q_hbm.1, f32[16,24]{1,0:T(8,128)} %target_ref.1, f32[16]{0:T(128)} %weight_ref.3, ...), custom_call_target="tpu_custom_call" | custom-call | flops 1610612736 | bytes 2359296 | tf_op jit(solution)/shard_map/pallas_call | solution.py:391
  41.7 3.5 %shard_map.113 = (f32[16,24,512]{2,1,0:T(8,128)}, f32[16,24,512]{2,1,0:T(8,128)}, f32[16,24,512]{2,1,0:T(8,128)}) custom-call(f32[16,24,512]{2,1,0:T(8,128)} %get-tuple-element.5.x_hbm, f32[16,24,512]{2,1,0:T(8,128)} %dual_hbm.3, f32[9,24,128]{2,1,0:T(8,128)} %get-tuple-element.6.packed_ref, f32[16]{0:T(128)} %weight_ref.3), custom_call_target="tpu_custom_call" | custom-call | flops 1966080 | bytes 3932160 | tf_op jit(solution)/shard_map/pallas_call | solution.py:417

commit v4 on v3

--- a/solution.py
+++ b/solution.py
@@ -23,9 +23,9 @@
 def kernel(
     nf, ns,
     anchor_hbm, cost_hbm, dual_hbm, q_hbm, target_ref, weight_ref, diag_ref, mask_ref, anc_ref,
-    x_hbm, packed_ref,
+    x_hbm, own_hbm, packed_ref,
     anchor_v, cost_v, dual_v, q_v, q_m, nat_b, nat, fixed_nat, xt, pre, fixed_t, q_t, gain_t, head_col,
-    x_out, small, total_w, same,
+    x_out, own_out, small, total_w, same,
     head_send, head_recv, note_send, note_recv, up_send, up_recv, down_send, down_recv, tail, front,
     in_sem, out_sem, head_ssem, head_rsem, note_ssem, note_rsem, up_ssem, up_rsem, down_ssem, down_rsem,
 ):
@@ -79,7 +79,6 @@
     def head_term(step):
         got = head_recv.at[step]
         pltpu.make_async_copy(got, got, head_rsem.at[step]).wait()
-        pltpu.make_async_copy(got, got, head_ssem.at[step]).wait()
         whole = head_send[step]
         for k in range(nf - 1):
             whole = whole + head_recv[step, k]
@@ -203,11 +202,9 @@
         in_first = (own_id == first_id).astype(F32)
         in_last = (own_id == last_id).astype(F32)
         scale = 1.0 / (total_w[l] + in_first * left_w + in_last * right_w)
-        packed = jnp.where(column == l, scale, packed)
-        packed = jnp.where(column == leaves + l, in_first * goes_back * scale, packed)
-        packed = jnp.where(column == 2 * leaves + l, in_last * scale, packed)
-        if l > 0:
-            packed = jnp.where(column == 3 * leaves + l, same[l], packed)
+        total_w[l] = scale
+        packed = jnp.where(column == l, in_first * goes_back * scale, packed)
+        packed = jnp.where(column == leaves + l, in_last * scale, packed)
     packed_ref[2 * node_blocks] = packed
 
     lax.fori_loop(5, PROX_ITERS, advance, 0)
@@ -247,6 +244,7 @@
                 run = weighted + same[l] * run
                 in_first = in_first * same[l]
                 opening = opening + in_first * weighted
+            own_out[l, :, lanes(c)] = run
         opening = opening * goes_back
         tail[c] = run
         front[c] = opening
@@ -263,6 +261,14 @@
 
     store_x = pltpu.make_async_copy(x_out, x_hbm, out_sem.at[0])
     store_x.start()
+    for c in range(node_blocks):
+        run = tail[c]
+        for l in range(leaves - 1, -1, -1):
+            if l < leaves - 1:
+                run = jnp.where(same[l + 1] > 0.5, run, own_out[l, :, lanes(c)])
+            own_out[l, :, lanes(c)] = run * total_w[l]
+    store_own = pltpu.make_async_copy(own_out, own_hbm, out_sem.at[1])
+    store_own.start()
 
     def upward():
         for c in range(node_blocks):
@@ -317,59 +323,60 @@
         def _():
             down_copy(c).wait_send()
 
+    for step in range(PROX_ITERS):
+        pltpu.make_async_copy(head_recv.at[step], head_recv.at[step], head_ssem.at[step]).wait()
     store_x.wait()
+    store_own.wait()
 
 
 def finish(
-    x_hbm, dual_hbm, packed_ref, weight_ref,
+    x_hbm, own_hbm, dual_hbm, packed_ref,
     xout_hbm, avg_hbm, newdual_hbm,
-    x_v, dual_v, avg_v, new_v, coef, in_sem, out_sem,
+    x_v, own_v, dual_v, coef, in_sem, out_sem,
 ):
     leaves, sections, nodes = x_hbm.shape
     node_blocks = nodes // LANES
-
-    def lanes(block):
-        return pl.ds(block * LANES, LANES)
-
-    def load(c):
+    group = 4
+    groups = leaves // group
+
+    def moves(g, pairs, sem):
+        some = pl.ds(g * group, group)
         return [
-            pltpu.make_async_copy(src.at[:, :, lanes(c)], dst.at[:, :, lanes(c)], in_sem.at[2 * c + i])
-            for i, (src, dst) in enumerate(((x_hbm, x_v), (dual_hbm, dual_v)))
+            pltpu.make_async_copy(src.at[some], dst.at[some], sem.at[3 * g + i])
+            for i, (src, dst) in enumerate(pairs)
         ]
 
-    def store(c):
-        return [
-            pltpu.make_async_copy(src.at[:, :, lanes(c)], dst.at[:, :, lanes(c)], out_sem.at[3 * c + i])
-            for i, (src, dst) in enumerate(((x_v, xout_hbm), (avg_v, avg_hbm), (new_v, newdual_hbm)))
-        ]
-
-    for c in range(node_blocks):
-        for copy in load(c):
+    def load(g):
+        return moves(g, ((x_hbm, x_v), (own_hbm, own_v), (dual_hbm, dual_v)), in_sem)
+
+    def store(g):
+        return moves(g, ((x_v, xout_hbm), (own_v, avg_hbm), (dual_v, newdual_hbm)), out_sem)
+
+    for g in range(groups):
+        for copy in load(g):
             copy.start()
     packed = packed_ref[2 * node_blocks]
-    for i in range(4 * leaves):
+    for i in range(2 * leaves):
         coef[i] = jnp.broadcast_to(packed[:, i : i + 1], (sections, LANES))
-    scale, left, right, same = (lambda l, i=i: coef[i * leaves + l] for i in range(4))
-    for c in range(node_blocks):
-        from_x, from_dual = load(c)
-        from_x.wait()
-        run = weight_ref[0] * x_v[0, :, lanes(c)]
-        avg_v[0, :, lanes(c)] = run
-        for l in range(1, leaves):
-            run = weight_ref[l] * x_v[l, :, lanes(c)] + same(l) * run
-            avg_v[l, :, lanes(c)] = run
-        from_dual.wait()
-        total = run
-        for l in range(leaves - 1, -1, -1):
-            if l < leaves - 1:
-                total = jnp.where(same(l + 1) > 0.5, total, avg_v[l, :, lanes(c)])
-            average = total * scale(l) + left(l) * packed_ref[c] + right(l) * packed_ref[node_blocks + c]
-            avg_v[l, :, lanes(c)] = average
-            new_v[l, :, lanes(c)] = dual_v[l, :, lanes(c)] + penalty * (x_v[l, :, lanes(c)] - average)
-        for copy in store(c):
+    for g in range(groups):
+        for copy in load(g):
+            copy.wait()
+        stores = store(g)
+        stores[0].start()
+        for l in range(g * group, (g + 1) * group):
+            for c in range(node_blocks):
+                some = pl.ds(c * LANES, LANES)
+                average = (
+                    own_v[l, :, some]
+                    + coef[l] * packed_ref[c]
+                    + coef[leaves + l] * packed_ref[node_blocks + c]
+                )
+                own_v[l, :, some] = average
+                dual_v[l, :, some] = dual_v[l, :, some] + penalty * (x_v[l, :, some] - average)
+        for copy in stores[1:]:
             copy.start()
-    for c in range(node_blocks):
-        for copy in store(c):
+    for g in range(groups):
+        for copy in store(g):
             copy.wait()
 
 
@@ -383,28 +390,29 @@
     coef = (leaves, sections, LANES)
     piece = (blocks, sections, LANES)
     out = jax.ShapeDtypeStruct(cube, F32)
+    hbm = pl.BlockSpec(memory_space=pltpu.HBM)
     far = pl.BlockSpec(memory_space=pl.ANY)
     near = pl.BlockSpec(memory_space=vmem)
     scalars = pl.BlockSpec(memory_space=smem)
     packed = jax.ShapeDtypeStruct((2 * blocks + 1, sections, LANES), F32)
-    limit = 56 * 1024 * 1024
-    state, parts = pl.pallas_call(
+    limit = 24 * 1024 * 1024
+    state, own, parts = pl.pallas_call(
         functools.partial(kernel, nf, ns),
-        out_shape=(out, packed),
-        in_specs=[far, far, far, far, near, scalars, near, scalars, near],
-        out_specs=(far, near),
+        out_shape=(out, out, packed),
+        in_specs=[hbm, hbm, hbm, hbm, near, scalars, near, scalars, near],
+        out_specs=(far, far, near),
         scratch_shapes=[
             vmem(cube, BF16), vmem(cube, BF16), vmem(cube, F32), vmem((nodes, nodes), BF16),
             vmem((nodes, nodes), BF16), vmem((rows, nodes), BF16), vmem((rows, nodes), F32), vmem((rows, nodes), F32),
             vmem((nodes, rows), F32), vmem((nodes, rows), F32), vmem((nodes, rows), F32),
             vmem((nodes, nodes), BF16), vmem((nodes, LANES), F32), vmem((rows, LANES), F32),
-            vmem(cube, F32), vmem((LANES, LANES), F32),
+            vmem(cube, F32), vmem(cube, F32), vmem((LANES, LANES), F32),
             vmem(coef, F32), vmem(coef, F32),
             vmem((PROX_ITERS, 1, rows), F32), vmem((PROX_ITERS, nf - 1, 1, rows), F32),
             vmem((sections, LANES), F32), vmem((ns - 1, sections, LANES), F32),
             vmem(piece, F32), vmem(piece, F32), vmem(piece, F32), vmem(piece, F32),
             vmem(piece, F32), vmem(piece, F32),
-            dma((4,)), dma((1,)), dma((PROX_ITERS,)), dma((PROX_ITERS,)), dma, dma,
+            dma((4,)), dma((2,)), dma((PROX_ITERS,)), dma((PROX_ITERS,)), dma, dma,
             dma((blocks,)), dma((blocks,)), dma((blocks,)), dma((blocks,)),
         ],
         compiler_params=pltpu.CompilerParams(
@@ -413,19 +421,19 @@
         cost_estimate=pl.CostEstimate(
             flops=2 * PROX_ITERS * rows * nodes * nodes, bytes_accessed=12 * rows * nodes, transcendentals=0
         ),
-    )(anchor, cost_lin, dual, q_mat, target, leaf_weight, diag_gain.reshape(1, nodes), block_mask, ancestor.T)
+    )(*(pltpu.with_memory_space_constraint(v, pltpu.HBM) for v in (anchor, cost_lin, dual, q_mat)), target, leaf_weight, diag_gain.reshape(1, nodes), block_mask, ancestor.T)
     return pl.pallas_call(
         finish,
         out_shape=(out, out, out),
-        in_specs=[far, far, near, scalars],
+        in_specs=[far, far, far, near],
         out_specs=(far, far, far),
         scratch_shapes=[
-            vmem(cube, F32), vmem(cube, F32), vmem(cube, F32), vmem(cube, F32),
-            vmem((4 * leaves, sections, LANES), F32), dma((2 * blocks,)), dma((3 * blocks,)),
+            vmem(cube, F32), vmem(cube, F32), vmem(cube, F32),
+            vmem((2 * leaves, sections, LANES), F32), dma((3 * leaves // 4,)), dma((3 * leaves // 4,)),
         ],
         compiler_params=pltpu.CompilerParams(vmem_limit_bytes=limit),
-        cost_estimate=pl.CostEstimate(flops=10 * rows * nodes, bytes_accessed=20 * rows * nodes, transcendentals=0),
-    )(state, dual, parts, leaf_weight)
+        cost_estimate=pl.CostEstimate(flops=8 * rows * nodes, bytes_accessed=24 * rows * nodes, transcendentals=0),
+    )(state, own, dual, parts)
 
 
 def solution(mesh):

time: 45.4 us -> 48.7 us (1.073)
  local copies, waits for them, and re-layouts: 0 us -> 2.75 us
  Pallas kernels: 44.5 us -> 45 us
    unnamed x0 -> x12, local copies, waits for them, and re-layouts: none -> 2.75 us
where the time goes in v4:
time: 48.7 us; the launch traced here: 48.4 us
  Pallas kernels  45 us (92%)
  local copies, waits for them, and re-layouts  2.75 us (6%)
  between operations  0.67 us (1%)
    pallas_call x1, Pallas kernels, local(): pl.pallas_call(functools.partial(kernel, nf, ns), out_shape=(out, out, pa...  40.1 us
    pallas_call x1, Pallas kernels, local(): pl.pallas_call(finish, out_shape=(out, out, out), in_specs=[far, far, far...  4.85 us
    unnamed x12, local copies, waits for them, and re-layouts  2.75 us

profile of v4, /device:TPU:0, one launch (start us, length us, event | category | flops | bytes accessed | tf_op | source)
XLA Modules:
  0.0 48.4 jit_solution(2027944332281772483)
XLA Ops:
  0.6 0.0 copy-start.3
  0.6 0.0 copy-start.5
  0.7 0.7 %copy-done.3 = f32[512]{0:T(512)S(1)} copy-done((f32[512]{0:T(512)S(1)}, f32[512]{0:T(512)}, u32[]{:S(2)}) %copy-start.3) | copy-done | bytes 2072
  1.3 0.0 copy-done.5
  1.3 0.0 copy-start.1
  1.3 0.7 %copy-done.1 = f32[16,24]{1,0:T(8,128)S(1)} copy-done((f32[16,24]{1,0:T(8,128)S(1)}, f32[16,24]{1,0:T(8,128)}, u32[]{:S(2)}) %copy-start.1) | copy-done | bytes 1560
  2.0 0.0 copy-start.2
  2.0 0.7 %copy-done.2 = s32[24,16]{0,1:T(8,128)S(1)} copy-done((s32[24,16]{0,1:T(8,128)S(1)}, s32[24,16]{0,1:T(8,128)}, u32[]{:S(2)}) %copy-start.2) | copy-done | bytes 1560
  2.7 0.0 copy-start.4
  2.7 0.7 %copy-done.4 = s32[1,4,4]{2,1,0:T(4,128)S(1)} copy-done((s32[1,4,4]{2,1,0:T(4,128)S(1)}, s32[1,4,4]{2,1,0:T(4,128)}, u32[]{:S(2)}) %copy-start.4) | copy-done | bytes 88
  3.4 0.0 copy-start
  3.4 40.1 %shard_map.112 = (f32[16,24,512]{2,1,0:T(8,128)S(1)}, f32[16,24,512]{2,1,0:T(8,128)S(1)}, f32[9,24,128]{2,1,0:T(8,128)S(1)}) custom-call(bf16[16,24,512]{2,1,0:T(8,128)(2,1)} %anchor_hbm.1, bf16[16,24,512]{2,1,0:T(8,128)(2,1)} %cost_hbm.1, f32[16,24,512]{2,1,0:T(8,128)} %dual_hbm.3, bf16[512,512]{1,0:T(8,128)(2,1)} %q_hbm.1, f32[16,24]{1,0:T(8,128)S(1)} %copy-done.1, ...), custom_call_target="tpu_custom_call" | custom-call | flops 1610612736 | bytes 2359296 | tf_op jit(solution)/shard_map/pallas_call | solution.py:399
  43.5 0.0 copy-done
  43.5 4.9 %shard_map.113 = (f32[16,24,512]{2,1,0:T(8,128)}, f32[16,24,512]{2,1,0:T(8,128)}, f32[16,24,512]{2,1,0:T(8,128)}) custom-call(f32[16,24,512]{2,1,0:T(8,128)S(1)} %get-tuple-element.6.x_hbm, f32[16,24,512]{2,1,0:T(8,128)S(1)} %get-tuple-element.7.own_hbm, f32[16,24,512]{2,1,0:T(8,128)S(1)} %copy-done, f32[9,24,128]{2,1,0:T(8,128)S(1)} %get-tuple-element.8.packed_ref), custom_call_target="tpu_custom_call" | custom-call | flops 1572864 | bytes 4718592 | tf_op jit(solution)/shard_map/pallas_call | solution.py:425
Async XLA Ops:
  0.6 0.7 %copy-start.3 = (f32[512]{0:T(512)S(1)}, f32[512]{0:T(512)}, u32[]{:S(2)}) copy-start(f32[512]{0:T(512)} %param.15) | copy-start | bytes 6148
  0.6 0.7 %copy-start.5 = (f32[16]{0:T(128)S(1)}, f32[16]{0:T(128)}, u32[]{:S(2)}) copy-start(f32[16]{0:T(128)} %weight_ref.1) | copy-start | bytes 196
  1.3 0.7 %copy-start.1 = (f32[16,24]{1,0:T(8,128)S(1)}, f32[16,24]{1,0:T(8,128)}, u32[]{:S(2)}) copy-start(f32[16,24]{1,0:T(8,128)} %target_ref.1) | copy-start | bytes 4612
  2.0 0.7 %copy-start.2 = (s32[24,16]{0,1:T(8,128)S(1)}, s32[24,16]{0,1:T(8,128)}, u32[]{:S(2)}) copy-start(s32[24,16]{0,1:T(8,128)} %param.17) | copy-start | bytes 4612
  2.7 0.7 %copy-start.4 = (s32[1,4,4]{2,1,0:T(4,128)S(1)}, s32[1,4,4]{2,1,0:T(4,128)}, u32[]{:S(2)}) copy-start(s32[1,4,4]{2,1,0:T(4,128)} %mask_ref.1) | copy-start | bytes 196
  3.4 40.1 %copy-start = (f32[16,24,512]{2,1,0:T(8,128)S(1)}, f32[16,24,512]{2,1,0:T(8,128)}, u32[]{:S(2)}) copy-start(f32[16,24,512]{2,1,0:T(8,128)} %dual_hbm.3) | copy-start | bytes 2359300

commit v5 on v4

--- a/solution.py
+++ b/solution.py
@@ -22,14 +22,15 @@
 
 def kernel(
     nf, ns,
-    anchor_hbm, cost_hbm, dual_hbm, q_hbm, target_ref, weight_ref, diag_ref, mask_ref, anc_ref,
-    x_hbm, own_hbm, packed_ref,
+    anchor_hbm, cost_hbm, dual_hbm, q_hbm, target_hbm, weight_hbm, diag_hbm, mask_hbm, anc_hbm,
+    x_out, own_out, packed_ref,
+    target_ref, weight_ref, diag_ref, mask_ref, anc_ref,
     anchor_v, cost_v, dual_v, q_v, q_m, nat_b, nat, fixed_nat, xt, pre, fixed_t, q_t, gain_t, head_col,
-    x_out, own_out, small, total_w, same,
+    small, total_w, same,
     head_send, head_recv, note_send, note_recv, up_send, up_recv, down_send, down_recv, tail, front,
-    in_sem, out_sem, head_ssem, head_rsem, note_ssem, note_rsem, up_ssem, up_rsem, down_ssem, down_rsem,
+    in_sem, head_ssem, head_rsem, note_ssem, note_rsem, up_ssem, up_rsem, down_ssem, down_rsem,
 ):
-    leaves, sections, nodes = x_hbm.shape
+    leaves, sections, nodes = x_out.shape
     rows = leaves * sections
     lane_blocks = rows // LANES
     node_blocks = nodes // LANES
@@ -53,7 +54,11 @@
     loads = [
         pltpu.make_async_copy(src, dst, in_sem.at[i])
         for i, (src, dst) in enumerate(
-            ((anchor_hbm, anchor_v), (q_hbm, q_v), (cost_hbm, cost_v), (dual_hbm, dual_v))
+            (
+                (anchor_hbm, anchor_v), (q_hbm, q_v), (cost_hbm, cost_v), (dual_hbm, dual_v),
+                (target_hbm, target_ref), (weight_hbm, weight_ref), (diag_hbm, diag_ref),
+                (mask_hbm, mask_ref), (anc_hbm, anc_ref),
+            )
         )
     ]
     for load in loads:
@@ -100,6 +105,8 @@
     pl.semaphore_wait(barrier, nf - 1 + ns - 1)
     send_heads(0)
 
+    for load in loads[4:]:
+        load.wait()
     small[...] = jnp.zeros_like(small)
     small[0:leaves, 0:sections] = anc_ref[...].astype(F32)
     small[leaves : 2 * leaves, 0:sections] = target_ref[...]
@@ -259,16 +266,12 @@
             down_send[c] = opening
             down_copy(c).start()
 
-    store_x = pltpu.make_async_copy(x_out, x_hbm, out_sem.at[0])
-    store_x.start()
     for c in range(node_blocks):
         run = tail[c]
         for l in range(leaves - 1, -1, -1):
             if l < leaves - 1:
                 run = jnp.where(same[l + 1] > 0.5, run, own_out[l, :, lanes(c)])
             own_out[l, :, lanes(c)] = run * total_w[l]
-    store_own = pltpu.make_async_copy(own_out, own_hbm, out_sem.at[1])
-    store_own.start()
 
     def upward():
         for c in range(node_blocks):
@@ -325,59 +328,40 @@
 
     for step in range(PROX_ITERS):
         pltpu.make_async_copy(head_recv.at[step], head_recv.at[step], head_ssem.at[step]).wait()
-    store_x.wait()
-    store_own.wait()
-
-
-def finish(
-    x_hbm, own_hbm, dual_hbm, packed_ref,
-    xout_hbm, avg_hbm, newdual_hbm,
-    x_v, own_v, dual_v, coef, in_sem, out_sem,
-):
-    leaves, sections, nodes = x_hbm.shape
+
+
+def finish(x_ref, own_ref, dual_ref, packed_ref, xout_hbm, avg_hbm, newdual_hbm, avg_v, new_v, coef, out_sem):
+    leaves, sections, nodes = x_ref.shape
     node_blocks = nodes // LANES
     group = 4
-    groups = leaves // group
-
-    def moves(g, pairs, sem):
-        some = pl.ds(g * group, group)
-        return [
-            pltpu.make_async_copy(src.at[some], dst.at[some], sem.at[3 * g + i])
-            for i, (src, dst) in enumerate(pairs)
-        ]
-
-    def load(g):
-        return moves(g, ((x_hbm, x_v), (own_hbm, own_v), (dual_hbm, dual_v)), in_sem)
-
-    def store(g):
-        return moves(g, ((x_v, xout_hbm), (own_v, avg_hbm), (dual_v, newdual_hbm)), out_sem)
-
-    for g in range(groups):
-        for copy in load(g):
-            copy.start()
+
+    def store(first, i, src, dst):
+        some = pl.ds(first, group)
+        return pltpu.make_async_copy(src.at[some], dst.at[some], out_sem.at[3 * (first // group) + i])
+
+    stores = [store(l, 0, x_ref, xout_hbm) for l in range(0, leaves, group)]
+    for copy in stores:
+        copy.start()
     packed = packed_ref[2 * node_blocks]
     for i in range(2 * leaves):
         coef[i] = jnp.broadcast_to(packed[:, i : i + 1], (sections, LANES))
-    for g in range(groups):
-        for copy in load(g):
-            copy.wait()
-        stores = store(g)
-        stores[0].start()
-        for l in range(g * group, (g + 1) * group):
-            for c in range(node_blocks):
-                some = pl.ds(c * LANES, LANES)
-                average = (
-                    own_v[l, :, some]
-                    + coef[l] * packed_ref[c]
-                    + coef[leaves + l] * packed_ref[node_blocks + c]
-                )
-                own_v[l, :, some] = average
-                dual_v[l, :, some] = dual_v[l, :, some] + penalty * (x_v[l, :, some] - average)
-        for copy in stores[1:]:
-            copy.start()
-    for g in range(groups):
-        for copy in store(g):
-            copy.wait()
+    for l in range(leaves):
+        for c in range(node_blocks):
+            some = pl.ds(c * LANES, LANES)
+            average = (
+                own_ref[l, :, some]
+                + coef[l] * packed_ref[c]
+                + coef[leaves + l] * packed_ref[node_blocks + c]
+            )
+            avg_v[l, :, some] = average
+            new_v[l, :, some] = dual_ref[l, :, some] + penalty * (x_ref[l, :, some] - average)
+        if l % group == group - 1:
+            first = l - group + 1
+            for copy in (store(first, 1, avg_v, avg_hbm), store(first, 2, new_v, newdual_hbm)):
+                copy.start()
+                stores.append(copy)
+    for copy in stores:
+        copy.wait()
 
 
 def local(nf, ns, anchor, cost_lin, dual, target, leaf_weight, q_mat, diag_gain, block_mask, ancestor):
@@ -393,26 +377,27 @@
     hbm = pl.BlockSpec(memory_space=pltpu.HBM)
     far = pl.BlockSpec(memory_space=pl.ANY)
     near = pl.BlockSpec(memory_space=vmem)
-    scalars = pl.BlockSpec(memory_space=smem)
     packed = jax.ShapeDtypeStruct((2 * blocks + 1, sections, LANES), F32)
     limit = 24 * 1024 * 1024
     state, own, parts = pl.pallas_call(
         functools.partial(kernel, nf, ns),
         out_shape=(out, out, packed),
-        in_specs=[hbm, hbm, hbm, hbm, near, scalars, near, scalars, near],
-        out_specs=(far, far, near),
+        in_specs=[hbm] * 9,
+        out_specs=(near, near, near),
         scratch_shapes=[
+            vmem((leaves, sections), F32), smem((leaves,), F32), vmem((1, nodes), F32),
+            smem(block_mask.shape, jnp.int32), vmem((leaves, sections), jnp.int32),
             vmem(cube, BF16), vmem(cube, BF16), vmem(cube, F32), vmem((nodes, nodes), BF16),
             vmem((nodes, nodes), BF16), vmem((rows, nodes), BF16), vmem((rows, nodes), F32), vmem((rows, nodes), F32),
             vmem((nodes, rows), F32), vmem((nodes, rows), F32), vmem((nodes, rows), F32),
             vmem((nodes, nodes), BF16), vmem((nodes, LANES), F32), vmem((rows, LANES), F32),
-            vmem(cube, F32), vmem(cube, F32), vmem((LANES, LANES), F32),
+            vmem((LANES, LANES), F32),
             vmem(coef, F32), vmem(coef, F32),
             vmem((PROX_ITERS, 1, rows), F32), vmem((PROX_ITERS, nf - 1, 1, rows), F32),
             vmem((sections, LANES), F32), vmem((ns - 1, sections, LANES), F32),
             vmem(piece, F32), vmem(piece, F32), vmem(piece, F32), vmem(piece, F32),
             vmem(piece, F32), vmem(piece, F32),
-            dma((4,)), dma((2,)), dma((PROX_ITERS,)), dma((PROX_ITERS,)), dma, dma,
+            dma((9,)), dma((PROX_ITERS,)), dma((PROX_ITERS,)), dma, dma,
             dma((blocks,)), dma((blocks,)), dma((blocks,)), dma((blocks,)),
         ],
         compiler_params=pltpu.CompilerParams(
@@ -421,15 +406,22 @@
         cost_estimate=pl.CostEstimate(
             flops=2 * PROX_ITERS * rows * nodes * nodes, bytes_accessed=12 * rows * nodes, transcendentals=0
         ),
-    )(*(pltpu.with_memory_space_constraint(v, pltpu.HBM) for v in (anchor, cost_lin, dual, q_mat)), target, leaf_weight, diag_gain.reshape(1, nodes), block_mask, ancestor.T)
+    )(
+        *(
+            pltpu.with_memory_space_constraint(array, pltpu.HBM)
+            for array in (
+                anchor, cost_lin, dual, q_mat, target, leaf_weight, diag_gain.reshape(1, nodes), block_mask,
+                ancestor.T,
+            )
+        )
+    )
     return pl.pallas_call(
         finish,
         out_shape=(out, out, out),
-        in_specs=[far, far, far, near],
+        in_specs=[near, near, near, near],
         out_specs=(far, far, far),
         scratch_shapes=[
-            vmem(cube, F32), vmem(cube, F32), vmem(cube, F32),
-            vmem((2 * leaves, sections, LANES), F32), dma((3 * leaves // 4,)), dma((3 * leaves // 4,)),
+            vmem(cube, F32), vmem(cube, F32), vmem((2 * leaves, sections, LANES), F32), dma((3 * leaves // 4,)),
         ],
         compiler_params=pltpu.CompilerParams(vmem_limit_bytes=limit),
         cost_estimate=pl.CostEstimate(flops=8 * rows * nodes, bytes_accessed=24 * rows * nodes, transcendentals=0),

time: 48.7 us -> 41.9 us (0.86)
  Pallas kernels: 45 us -> 41.1 us
  local copies, waits for them, and re-layouts: 2.75 us -> 0.01 us
    pallas_call x1, Pallas kernels: 4.85 us -> 1.5 us  [local(): pl.pallas_call(finish, out_shape=(out, out, out), in_specs=[near, near, n...]
    unnamed x12 -> x2, local copies, waits for them, and re-layouts: 2.75 us -> 0.01 us
    pallas_call x1, Pallas kernels: 40.1 us -> 39.6 us  [local(): pl.pallas_call(functools.partial(kernel, nf, ns), out_shape=(out, out, pa...]
where the time goes in v5:
time: 41.9 us; the launch traced here: 41.7 us
  Pallas kernels  41.1 us (98%)
  between operations  0.66 us (2%)
    pallas_call x1, Pallas kernels, local(): pl.pallas_call(functools.partial(kernel, nf, ns), out_shape=(out, out, pa...  39.6 us
    pallas_call x1, Pallas kernels, local(): pl.pallas_call(finish, out_shape=(out, out, out), in_specs=[near, near, n...  1.5 us

profile of v5, /device:TPU:0, one launch (start us, length us, event | category | flops | bytes accessed | tf_op | source)
XLA Modules:
  0.0 41.7 jit_solution(6865364109041287095)
XLA Ops:
  0.6 0.0 copy-start
  0.6 39.6 %shard_map.112 = (f32[16,24,512]{2,1,0:T(8,128)S(1)}, f32[16,24,512]{2,1,0:T(8,128)S(1)}, f32[9,24,128]{2,1,0:T(8,128)S(1)}) custom-call(bf16[16,24,512]{2,1,0:T(8,128)(2,1)} %anchor_hbm.1, bf16[16,24,512]{2,1,0:T(8,128)(2,1)} %cost_hbm.1, f32[16,24,512]{2,1,0:T(8,128)} %dual_ref.1, bf16[512,512]{1,0:T(8,128)(2,1)} %q_hbm.1, f32[16,24]{1,0:T(8,128)} %target_hbm.1, ...), custom_call_target="tpu_custom_call" | custom-call | flops 1610612736 | bytes 2359296 | tf_op jit(solution)/shard_map/pallas_call | solution.py:382
  40.2 0.0 copy-done
  40.2 1.5 %shard_map.113 = (f32[16,24,512]{2,1,0:T(8,128)}, f32[16,24,512]{2,1,0:T(8,128)}, f32[16,24,512]{2,1,0:T(8,128)}) custom-call(f32[16,24,512]{2,1,0:T(8,128)S(1)} %get-tuple-element.6.x_ref, f32[16,24,512]{2,1,0:T(8,128)S(1)} %get-tuple-element.7.own_ref, f32[16,24,512]{2,1,0:T(8,128)S(1)} %copy-done, f32[9,24,128]{2,1,0:T(8,128)S(1)} %get-tuple-element.8.packed_ref), custom_call_target="tpu_custom_call" | custom-call | flops 1572864 | bytes 4718592 | tf_op jit(solution)/shard_map/pallas_call | solution.py:418
Async XLA Ops:
  0.6 39.6 %copy-start = (f32[16,24,512]{2,1,0:T(8,128)S(1)}, f32[16,24,512]{2,1,0:T(8,128)}, u32[]{:S(2)}) copy-start(f32[16,24,512]{2,1,0:T(8,128)} %dual_ref.1) | copy-start | bytes 2359300

commit v6 on v5

--- a/solution.py
+++ b/solution.py
@@ -23,9 +23,9 @@
 def kernel(
     nf, ns,
     anchor_hbm, cost_hbm, dual_hbm, q_hbm, target_hbm, weight_hbm, diag_hbm, mask_hbm, anc_hbm,
-    x_out, own_out, packed_ref,
+    x_out, own_out, ends_out, coef_out,
     target_ref, weight_ref, diag_ref, mask_ref, anc_ref,
-    anchor_v, cost_v, dual_v, q_v, q_m, nat_b, nat, fixed_nat, xt, pre, fixed_t, q_t, gain_t, head_col,
+    anchor_v, cost_v, dual_v, q_v, q_m, nat_b, nat, fixed_nat, xt, xb, pre, fixed_t, q_t, gain_t, head_col,
     small, total_w, same,
     head_send, head_recv, note_send, note_recv, up_send, up_recv, down_send, down_recv, tail, front,
     in_sem, head_ssem, head_rsem, note_ssem, note_rsem, up_ssem, up_rsem, down_ssem, down_rsem,
@@ -45,10 +45,11 @@
         return other
 
     order = sorted(range(1, nf), key=lambda k: -bin(k >> 1).count("1"))
+    partners = {k: partner(k) for k in order}
 
     barrier = pltpu.get_barrier_semaphore()
     for k in range(1, nf):
-        pl.semaphore_signal(barrier, inc=1, device_id=(partner(k), ms), device_id_type=MESH)
+        pl.semaphore_signal(barrier, inc=1, device_id=(partners[k], ms), device_id_type=MESH)
     for k in range(1, ns):
         pl.semaphore_signal(barrier, inc=1, device_id=(mf, lax.rem(ms + k, ns)), device_id_type=MESH)
     loads = [
@@ -77,7 +78,7 @@
                 dst_ref=head_recv.at[step, k - 1],
                 send_sem=head_ssem.at[step],
                 recv_sem=head_rsem.at[step],
-                device_id=(partner(k), ms),
+                device_id=(partners[k], ms),
                 device_id_type=MESH,
             ).start()
 
@@ -90,10 +91,14 @@
         return whole * (step_size * coupling / (nf * nodes))
 
     def window():
-        image = jnp.dot(q_t[...], xt[...].astype(BF16), preferred_element_type=F32)
-        for b in range(lane_blocks):
-            cols = slice(b * LANES, (b + 1) * LANES)
-            pre[:, cols] = gain_t[...] * xt[:, cols] - step_size * image[:, cols] - fixed_t[:, cols]
+        for first in range(0, rows, 2 * LANES):
+            last = min(first + 2 * LANES, rows)
+            image = jnp.dot(q_t[...], xb[:, first:last], preferred_element_type=F32)
+            for b in range(first, last, LANES):
+                cols = slice(b, b + LANES)
+                pre[:, cols] = (
+                    gain_t[...] * xt[:, cols] - step_size * image[:, b - first : b - first + LANES] - fixed_t[:, cols]
+                )
 
     loads[0].wait()
     for leaf in range(leaves):
@@ -137,6 +142,7 @@
             some = slice(b * 64, (b + 1) * 64)
             new = jnp.clip(pre[some, :] - term, -power_limit, power_limit)
             xt[some, :] = new
+            xb[some, :] = new.astype(BF16)
             part = part + jnp.sum(new.reshape(8, 8, rows), axis=0)
         head_send[step] = jnp.sum(part, axis=0, keepdims=True)
         send_heads(step)
@@ -203,16 +209,14 @@
         earlier = jnp.where(ms >= k, 1.0, 0.0)
         left_w += earlier * jnp.where(note[:, 1:2] == first_id, note[:, 0:1], 0.0)
         right_w += (1.0 - earlier) * jnp.where(note[:, 3:4] == last_id, note[:, 2:3], 0.0)
-    packed = jnp.zeros(wide, F32)
     for l in range(leaves):
         own_id = leaf_id(l)
         in_first = (own_id == first_id).astype(F32)
         in_last = (own_id == last_id).astype(F32)
         scale = 1.0 / (total_w[l] + in_first * left_w + in_last * right_w)
         total_w[l] = scale
-        packed = jnp.where(column == l, in_first * goes_back * scale, packed)
-        packed = jnp.where(column == leaves + l, in_last * scale, packed)
-    packed_ref[2 * node_blocks] = packed
+        coef_out[l] = in_first * goes_back * scale
+        coef_out[leaves + l] = in_last * scale
 
     lax.fori_loop(5, PROX_ITERS, advance, 0)
 
@@ -314,8 +318,8 @@
         upward()
 
     for c in range(node_blocks):
-        packed_ref[c] = up_recv[c]
-        packed_ref[node_blocks + c] = down_recv[c]
+        ends_out[c] = up_recv[c]
+        ends_out[node_blocks + c] = down_recv[c]
     for c in range(node_blocks):
 
         @pl.when(jnp.logical_not(at_top))
@@ -330,7 +334,7 @@
         pltpu.make_async_copy(head_recv.at[step], head_recv.at[step], head_ssem.at[step]).wait()
 
 
-def finish(x_ref, own_ref, dual_ref, packed_ref, xout_hbm, avg_hbm, newdual_hbm, avg_v, new_v, coef, out_sem):
+def finish(x_ref, own_ref, dual_ref, ends, coef, xout_hbm, avg_hbm, newdual_hbm, avg_v, new_v, out_sem):
     leaves, sections, nodes = x_ref.shape
     node_blocks = nodes // LANES
     group = 4
@@ -342,16 +346,11 @@
     stores = [store(l, 0, x_ref, xout_hbm) for l in range(0, leaves, group)]
     for copy in stores:
         copy.start()
-    packed = packed_ref[2 * node_blocks]
-    for i in range(2 * leaves):
-        coef[i] = jnp.broadcast_to(packed[:, i : i + 1], (sections, LANES))
     for l in range(leaves):
         for c in range(node_blocks):
             some = pl.ds(c * LANES, LANES)
             average = (
-                own_ref[l, :, some]
-                + coef[l] * packed_ref[c]
-                + coef[leaves + l] * packed_ref[node_blocks + c]
+                own_ref[l, :, some] + coef[l] * ends[c] + coef[leaves + l] * ends[node_blocks + c]
             )
             avg_v[l, :, some] = average
             new_v[l, :, some] = dual_ref[l, :, some] + penalty * (x_ref[l, :, some] - average)
@@ -377,19 +376,20 @@
     hbm = pl.BlockSpec(memory_space=pltpu.HBM)
     far = pl.BlockSpec(memory_space=pl.ANY)
     near = pl.BlockSpec(memory_space=vmem)
-    packed = jax.ShapeDtypeStruct((2 * blocks + 1, sections, LANES), F32)
+    sums = jax.ShapeDtypeStruct((2 * blocks, sections, LANES), F32)
+    shares = jax.ShapeDtypeStruct((2 * leaves, sections, LANES), F32)
     limit = 24 * 1024 * 1024
-    state, own, parts = pl.pallas_call(
+    state, own, parts, factors = pl.pallas_call(
         functools.partial(kernel, nf, ns),
-        out_shape=(out, out, packed),
+        out_shape=(out, out, sums, shares),
         in_specs=[hbm] * 9,
-        out_specs=(near, near, near),
+        out_specs=(near, near, near, near),
         scratch_shapes=[
             vmem((leaves, sections), F32), smem((leaves,), F32), vmem((1, nodes), F32),
             smem(block_mask.shape, jnp.int32), vmem((leaves, sections), jnp.int32),
             vmem(cube, BF16), vmem(cube, BF16), vmem(cube, F32), vmem((nodes, nodes), BF16),
             vmem((nodes, nodes), BF16), vmem((rows, nodes), BF16), vmem((rows, nodes), F32), vmem((rows, nodes), F32),
-            vmem((nodes, rows), F32), vmem((nodes, rows), F32), vmem((nodes, rows), F32),
+            vmem((nodes, rows), F32), vmem((nodes, rows), BF16), vmem((nodes, rows), F32), vmem((nodes, rows), F32),
             vmem((nodes, nodes), BF16), vmem((nodes, LANES), F32), vmem((rows, LANES), F32),
             vmem((LANES, LANES), F32),
             vmem(coef, F32), vmem(coef, F32),
@@ -418,14 +418,14 @@
     return pl.pallas_call(
         finish,
         out_shape=(out, out, out),
-        in_specs=[near, near, near, near],
+        in_specs=[near, near, near, near, near],
         out_specs=(far, far, far),
         scratch_shapes=[
-            vmem(cube, F32), vmem(cube, F32), vmem((2 * leaves, sections, LANES), F32), dma((3 * leaves // 4,)),
+            vmem(cube, F32), vmem(cube, F32), dma((3 * leaves // 4,)),
         ],
         compiler_params=pltpu.CompilerParams(vmem_limit_bytes=limit),
         cost_estimate=pl.CostEstimate(flops=8 * rows * nodes, bytes_accessed=24 * rows * nodes, transcendentals=0),
-    )(state, own, dual, parts)
+    )(state, own, dual, parts, factors)
 
 
 def solution(mesh):

time: 41.9 us -> 42 us (level)
  no operation moved by 1% of the time
where the time goes in v6:
time: 42 us; the launch traced here: 41.9 us
  Pallas kernels  41.2 us (98%)
  between operations  0.66 us (2%)
    pallas_call x1, Pallas kernels, local(): pl.pallas_call(functools.partial(kernel, nf, ns), out_shape=(out, out, su...  39.7 us
    pallas_call x1, Pallas kernels, local(): pl.pallas_call(finish, out_shape=(out, out, out), in_specs=[near, near, n...  1.49 us

profile of v6, /device:TPU:0, one launch (start us, length us, event | category | flops | bytes accessed | tf_op | source)
XLA Modules:
  0.0 41.9 jit_solution(14236401419261952000)
XLA Ops:
  0.6 0.0 copy-start
  0.6 39.7 %shard_map.112 = (f32[16,24,512]{2,1,0:T(8,128)S(1)}, f32[16,24,512]{2,1,0:T(8,128)S(1)}, f32[8,24,128]{2,1,0:T(8,128)S(1)}, f32[32,24,128]{2,1,0:T(8,128)S(1)}) custom-call(bf16[16,24,512]{2,1,0:T(8,128)(2,1)} %anchor_hbm.1, bf16[16,24,512]{2,1,0:T(8,128)(2,1)} %cost_hbm.1, f32[16,24,512]{2,1,0:T(8,128)} %dual_ref.1, bf16[512,512]{1,0:T(8,128)(2,1)} %q_hbm.1, ...), custom_call_target="tpu_custom_call" | custom-call | flops 1610612736 | bytes 2359296 | tf_op jit(solution)/shard_map/pallas_call | solution.py:382
  40.4 0.0 copy-done
  40.4 1.5 %shard_map.113 = (f32[16,24,512]{2,1,0:T(8,128)}, f32[16,24,512]{2,1,0:T(8,128)}, f32[16,24,512]{2,1,0:T(8,128)}) custom-call(f32[16,24,512]{2,1,0:T(8,128)S(1)} %get-tuple-element.7.x_ref, f32[16,24,512]{2,1,0:T(8,128)S(1)} %get-tuple-element.8.own_ref, f32[16,24,512]{2,1,0:T(8,128)S(1)} %copy-done, f32[8,24,128]{2,1,0:T(8,128)S(1)} %get-tuple-element.9.ends, ...), custom_call_target="tpu_custom_call" | custom-call | flops 1572864 | bytes 4718592 | tf_op jit(solution)/shard_map/pallas_call | solution.py:418
Async XLA Ops:
  0.6 39.8 %copy-start = (f32[16,24,512]{2,1,0:T(8,128)S(1)}, f32[16,24,512]{2,1,0:T(8,128)}, u32[]{:S(2)}) copy-start(f32[16,24,512]{2,1,0:T(8,128)} %dual_ref.1) | copy-start | bytes 2359300

commit v7 on v5

--- a/solution.py
+++ b/solution.py
@@ -27,8 +27,8 @@
     target_ref, weight_ref, diag_ref, mask_ref, anc_ref,
     anchor_v, cost_v, dual_v, q_v, q_m, nat_b, nat, fixed_nat, xt, pre, fixed_t, q_t, gain_t, head_col,
     small, total_w, same,
-    head_send, head_recv, note_send, note_recv, up_send, up_recv, down_send, down_recv, tail, front,
-    in_sem, head_ssem, head_rsem, note_ssem, note_rsem, up_ssem, up_rsem, down_ssem, down_rsem,
+    head_send, head_recv, head_all, note_send, note_recv, up_send, up_recv, down_send, down_recv, tail, front,
+    in_sem, head_ssem, head_rsem, all_rsem, note_ssem, note_rsem, up_ssem, up_rsem, down_ssem, down_rsem,
 ):
     leaves, sections, nodes = x_out.shape
     rows = leaves * sections
@@ -45,10 +45,11 @@
         return other
 
     order = sorted(range(1, nf), key=lambda k: -bin(k >> 1).count("1"))
+    partners = {k: partner(k) for k in order}
 
     barrier = pltpu.get_barrier_semaphore()
     for k in range(1, nf):
-        pl.semaphore_signal(barrier, inc=1, device_id=(partner(k), ms), device_id_type=MESH)
+        pl.semaphore_signal(barrier, inc=1, device_id=(partners[k], ms), device_id_type=MESH)
     for k in range(1, ns):
         pl.semaphore_signal(barrier, inc=1, device_id=(mf, lax.rem(ms + k, ns)), device_id_type=MESH)
     loads = [
@@ -70,24 +71,55 @@
     def lanes(block):
         return pl.ds(block * LANES, LANES)
 
+    second = lax.rem(mf, 2) == 1
+    first = jnp.logical_not(second)
+
     def send_heads(step):
-        for k in order:
+        def to(k):
             pltpu.make_async_remote_copy(
                 src_ref=head_send.at[step],
                 dst_ref=head_recv.at[step, k - 1],
                 send_sem=head_ssem.at[step],
                 recv_sem=head_rsem.at[step],
-                device_id=(partner(k), ms),
+                device_id=(partners[k], ms),
                 device_id_type=MESH,
             ).start()
 
+        @pl.when(first)
+        def _():
+            for k in order:
+                if k % 2 == 1:
+                    to(k)
+
+        @pl.when(second)
+        def _():
+            for k in order:
+                if k % 2 == 0:
+                    to(k)
+
     def head_term(step):
-        got = head_recv.at[step]
-        pltpu.make_async_copy(got, got, head_rsem.at[step]).wait()
-        whole = head_send[step]
-        for k in range(nf - 1):
-            whole = whole + head_recv[step, k]
-        return whole * (step_size * coupling / (nf * nodes))
+        @pl.when(second)
+        def _():
+            got = head_recv.at[step]
+            pltpu.make_async_copy(got, got, head_rsem.at[step]).wait()
+            whole = head_send[step]
+            for k in range(nf - 1):
+                whole = whole + head_recv[step, k]
+            head_all[step] = whole
+            pltpu.make_async_remote_copy(
+                src_ref=head_all.at[step],
+                dst_ref=head_all.at[step],
+                send_sem=head_ssem.at[step],
+                recv_sem=all_rsem.at[step],
+                device_id=(partners[1], ms),
+                device_id_type=MESH,
+            ).start()
+
+        @pl.when(first)
+        def _():
+            pltpu.make_async_copy(head_all.at[step], head_all.at[step], all_rsem.at[step]).wait()
+
+        return head_all[step] * (step_size * coupling / (nf * nodes))
 
     def window():
         image = jnp.dot(q_t[...], xt[...].astype(BF16), preferred_element_type=F32)
@@ -327,7 +359,8 @@
             down_copy(c).wait_send()
 
     for step in range(PROX_ITERS):
-        pltpu.make_async_copy(head_recv.at[step], head_recv.at[step], head_ssem.at[step]).wait()
+        sent = head_recv.at[step, pl.ds(0, nf // 2)]
+        pltpu.make_async_copy(sent, sent, head_ssem.at[step]).wait()
 
 
 def finish(x_ref, own_ref, dual_ref, packed_ref, xout_hbm, avg_hbm, newdual_hbm, avg_v, new_v, coef, out_sem):
@@ -394,10 +427,11 @@
             vmem((LANES, LANES), F32),
             vmem(coef, F32), vmem(coef, F32),
             vmem((PROX_ITERS, 1, rows), F32), vmem((PROX_ITERS, nf - 1, 1, rows), F32),
+            vmem((PROX_ITERS, 1, rows), F32),
             vmem((sections, LANES), F32), vmem((ns - 1, sections, LANES), F32),
             vmem(piece, F32), vmem(piece, F32), vmem(piece, F32), vmem(piece, F32),
             vmem(piece, F32), vmem(piece, F32),
-            dma((9,)), dma((PROX_ITERS,)), dma((PROX_ITERS,)), dma, dma,
+            dma((9,)), dma((PROX_ITERS,)), dma((PROX_ITERS,)), dma((PROX_ITERS,)), dma, dma,
             dma((blocks,)), dma((blocks,)), dma((blocks,)), dma((blocks,)),
         ],
         compiler_params=pltpu.CompilerParams(

time: 41.9 us -> 45.6 us (1.088)
  Pallas kernels: 41.1 us -> 44.8 us
    pallas_call x1, Pallas kernels: 39.6 us -> 43.3 us  [local(): pl.pallas_call(functools.partial(kernel, nf, ns), out_shape=(out, out, pa...]
where the time goes in v7:
time: 45.6 us; the launch traced here: 45.5 us
  Pallas kernels  44.8 us (98%)
  between operations  0.66 us (1%)
    pallas_call x1, Pallas kernels, local(): pl.pallas_call(functools.partial(kernel, nf, ns), out_shape=(out, out, pa...  43.3 us
    pallas_call x1, Pallas kernels, local(): pl.pallas_call(finish, out_shape=(out, out, out), in_specs=[near, near, n...  1.5 us

profile of v7, /device:TPU:0, one launch (start us, length us, event | category | flops | bytes accessed | tf_op | source)
XLA Modules:
  0.0 45.5 jit_solution(11555007603975654994)
XLA Ops:
  0.6 0.0 copy-start
  0.6 43.3 %shard_map.112 = (f32[16,24,512]{2,1,0:T(8,128)S(1)}, f32[16,24,512]{2,1,0:T(8,128)S(1)}, f32[9,24,128]{2,1,0:T(8,128)S(1)}) custom-call(bf16[16,24,512]{2,1,0:T(8,128)(2,1)} %anchor_hbm.1, bf16[16,24,512]{2,1,0:T(8,128)(2,1)} %cost_hbm.1, f32[16,24,512]{2,1,0:T(8,128)} %dual_ref.1, bf16[512,512]{1,0:T(8,128)(2,1)} %q_hbm.1, f32[16,24]{1,0:T(8,128)} %target_hbm.1, ...), custom_call_target="tpu_custom_call" | custom-call | flops 1610612736 | bytes 2359296 | tf_op jit(solution)/shard_map/pallas_call | solution.py:415
  44.0 0.0 copy-done
  44.0 1.5 %shard_map.113 = (f32[16,24,512]{2,1,0:T(8,128)}, f32[16,24,512]{2,1,0:T(8,128)}, f32[16,24,512]{2,1,0:T(8,128)}) custom-call(f32[16,24,512]{2,1,0:T(8,128)S(1)} %get-tuple-element.6.x_ref, f32[16,24,512]{2,1,0:T(8,128)S(1)} %get-tuple-element.7.own_ref, f32[16,24,512]{2,1,0:T(8,128)S(1)} %copy-done, f32[9,24,128]{2,1,0:T(8,128)S(1)} %get-tuple-element.8.packed_ref), custom_call_target="tpu_custom_call" | custom-call | flops 1572864 | bytes 4718592 | tf_op jit(solution)/shard_map/pallas_call | solution.py:452
Async XLA Ops:
  0.6 43.4 %copy-start = (f32[16,24,512]{2,1,0:T(8,128)S(1)}, f32[16,24,512]{2,1,0:T(8,128)}, u32[]{:S(2)}) copy-start(f32[16,24,512]{2,1,0:T(8,128)} %dual_ref.1) | copy-start | bytes 2359300

commit v8 on v5

--- a/solution.py
+++ b/solution.py
@@ -222,17 +222,21 @@
     for b in range(lane_blocks):
         head_col[lanes(b), :] = jnp.broadcast_to(term[:, b * LANES : (b + 1) * LANES], (LANES, LANES)).T
 
-    def up_copy(c):
+    half = node_blocks // 2
+
+    def up_copy(p):
+        some = pl.ds(p * half, half)
         return pltpu.make_async_remote_copy(
-            src_ref=up_send.at[c], dst_ref=up_recv.at[c],
-            send_sem=up_ssem.at[c], recv_sem=up_rsem.at[c],
+            src_ref=up_send.at[some], dst_ref=up_recv.at[some],
+            send_sem=up_ssem.at[p], recv_sem=up_rsem.at[p],
             device_id=(mf, lax.rem(ms + 1, ns)), device_id_type=MESH,
         )
 
-    def down_copy(c):
+    def down_copy(p):
+        some = pl.ds(p * half, half)
         return pltpu.make_async_remote_copy(
-            src_ref=down_send.at[c], dst_ref=down_recv.at[c],
-            send_sem=down_ssem.at[c], recv_sem=down_rsem.at[c],
+            src_ref=down_send.at[some], dst_ref=down_recv.at[some],
+            send_sem=down_ssem.at[p], recv_sem=down_rsem.at[p],
             device_id=(mf, lax.rem(ms + ns - 1, ns)), device_id_type=MESH,
         )
 
@@ -259,12 +263,14 @@
         @pl.when(at_bottom)
         def _():
             up_send[c] = run
-            up_copy(c).start()
+            if c % half == half - 1:
+                up_copy(c // half).start()
 
         @pl.when(at_top)
         def _():
             down_send[c] = opening
-            down_copy(c).start()
+            if c % half == half - 1:
+                down_copy(c // half).start()
 
     for c in range(node_blocks):
         run = tail[c]
@@ -274,22 +280,24 @@
             own_out[l, :, lanes(c)] = run * total_w[l]
 
     def upward():
-        for c in range(node_blocks):
-            up_copy(c).wait_recv()
+        for p in range(2):
+            up_copy(p).wait_recv()
 
             @pl.when(jnp.logical_not(at_top))
             def _():
-                up_send[c] = tail[c] + spans * up_recv[c]
-                up_copy(c).start()
+                for c in range(p * half, (p + 1) * half):
+                    up_send[c] = tail[c] + spans * up_recv[c]
+                up_copy(p).start()
 
     def downward():
-        for c in range(node_blocks):
-            down_copy(c).wait_recv()
+        for p in range(2):
+            down_copy(p).wait_recv()
 
             @pl.when(jnp.logical_not(at_bottom))
             def _():
-                down_send[c] = front[c] + spans * down_recv[c]
-                down_copy(c).start()
+                for c in range(p * half, (p + 1) * half):
+                    down_send[c] = front[c] + spans * down_recv[c]
+                down_copy(p).start()
 
     low = ms < ns // 2
 
@@ -316,15 +324,15 @@
     for c in range(node_blocks):
         packed_ref[c] = up_recv[c]
         packed_ref[node_blocks + c] = down_recv[c]
-    for c in range(node_blocks):
+    for p in range(2):
 
         @pl.when(jnp.logical_not(at_top))
         def _():
-            up_copy(c).wait_send()
+            up_copy(p).wait_send()
 
         @pl.when(jnp.logical_not(at_bottom))
         def _():
-            down_copy(c).wait_send()
+            down_copy(p).wait_send()
 
     for step in range(PROX_ITERS):
         pltpu.make_async_copy(head_recv.at[step], head_recv.at[step], head_ssem.at[step]).wait()
@@ -398,7 +406,7 @@
             vmem(piece, F32), vmem(piece, F32), vmem(piece, F32), vmem(piece, F32),
             vmem(piece, F32), vmem(piece, F32),
             dma((9,)), dma((PROX_ITERS,)), dma((PROX_ITERS,)), dma, dma,
-            dma((blocks,)), dma((blocks,)), dma((blocks,)), dma((blocks,)),
+            dma((2,)), dma((2,)), dma((2,)), dma((2,)),
         ],
         compiler_params=pltpu.CompilerParams(
             collective_id=0, has_side_effects=True, vmem_limit_bytes=limit

time: 41.9 us -> 42.2 us (level)
  no operation moved by 1% of the time
where the time goes in v8:
time: 42.2 us; the launch traced here: 42 us
  Pallas kernels  41.3 us (98%)
  between operations  0.66 us (2%)
    pallas_call x1, Pallas kernels, local(): pl.pallas_call(functools.partial(kernel, nf, ns), out_shape=(out, out, pa...  39.8 us
    pallas_call x1, Pallas kernels, local(): pl.pallas_call(finish, out_shape=(out, out, out), in_specs=[near, near, n...  1.5 us

profile of v8, /device:TPU:0, one launch (start us, length us, event | category | flops | bytes accessed | tf_op | source)
XLA Modules:
  0.0 42.0 jit_solution(17516662171761075945)
XLA Ops:
  0.6 0.0 copy-start
  0.6 39.8 %shard_map.112 = (f32[16,24,512]{2,1,0:T(8,128)S(1)}, f32[16,24,512]{2,1,0:T(8,128)S(1)}, f32[9,24,128]{2,1,0:T(8,128)S(1)}) custom-call(bf16[16,24,512]{2,1,0:T(8,128)(2,1)} %anchor_hbm.1, bf16[16,24,512]{2,1,0:T(8,128)(2,1)} %cost_hbm.1, f32[16,24,512]{2,1,0:T(8,128)} %dual_ref.1, bf16[512,512]{1,0:T(8,128)(2,1)} %q_hbm.1, f32[16,24]{1,0:T(8,128)} %target_hbm.1, ...), custom_call_target="tpu_custom_call" | custom-call | flops 1610612736 | bytes 2359296 | tf_op jit(solution)/shard_map/pallas_call | solution.py:390
  40.5 0.0 copy-done
  40.5 1.5 %shard_map.113 = (f32[16,24,512]{2,1,0:T(8,128)}, f32[16,24,512]{2,1,0:T(8,128)}, f32[16,24,512]{2,1,0:T(8,128)}) custom-call(f32[16,24,512]{2,1,0:T(8,128)S(1)} %get-tuple-element.6.x_ref, f32[16,24,512]{2,1,0:T(8,128)S(1)} %get-tuple-element.7.own_ref, f32[16,24,512]{2,1,0:T(8,128)S(1)} %copy-done, f32[9,24,128]{2,1,0:T(8,128)S(1)} %get-tuple-element.8.packed_ref), custom_call_target="tpu_custom_call" | custom-call | flops 1572864 | bytes 4718592 | tf_op jit(solution)/shard_map/pallas_call | solution.py:426
Async XLA Ops:
  0.6 39.9 %copy-start = (f32[16,24,512]{2,1,0:T(8,128)S(1)}, f32[16,24,512]{2,1,0:T(8,128)}, u32[]{:S(2)}) copy-start(f32[16,24,512]{2,1,0:T(8,128)} %dual_ref.1) | copy-start | bytes 2359300
